TPU v7x, 128 devices: a whole 4x4x4 slice. The times are simulated.
128 devices in a mesh: pipe: 8 (over y, z_lo), expert: 8 (over z_hi, x), dp: 2 (over core).
Axes of the slice: x: 4, y: 4, z: 4 (z_hi: 2, z_lo: 2; z = z_hi * 2 + z_lo), core: 2. Of those that a mesh axis runs over, the one named last changes fastest.
Arguments:
- rising_in: bfloat16 [8, 2048, 7168], P('pipe', ('expert', 'dp')), may hold values from -6 to 6
- rising_ids: int32 [8, 2048, 2], P('pipe', ('expert', 'dp')), may hold values from 0 to 7, all different within a row; in each aligned block of 128 rows (0 to 127, 128 to 255, ..., all dimensions but the last counted through in order) at most 40 rows name the same one
- rising_gates: float32 [8, 2048, 2], P('pipe', ('expert', 'dp')), may hold values from 0.1 to 1
- rising_drop: int32 [8, 2, 64], P('pipe', None, ('expert', 'dp')), may hold values from -2147483648 to 2147483647, as said below
- sinking_grad: bfloat16 [8, 2048, 7168], P('pipe', ('expert', 'dp')), may hold values from -6 to 6
- sinking_ids: int32 [8, 2048, 2], P('pipe', ('expert', 'dp')), may hold values from 0 to 7, all different within a row; in each aligned block of 128 rows (0 to 127, 128 to 255, ..., all dimensions but the last counted through in order) at most 40 rows name the same one
- sinking_gates: float32 [8, 2048, 2], P('pipe', ('expert', 'dp')), may hold values from 0.1 to 1
- sinking_drop: int32 [8, 2, 64], P('pipe', None, ('expert', 'dp')), may hold values from -2147483648 to 2147483647, as said below
- sinking_pre: bfloat16 [8, 8, 640, 1024], P('pipe', 'expert', None, 'dp'), may hold values from -6 to 6
- w_in: bfloat16 [8, 8, 7168, 1024], P('pipe', 'expert', None, 'dp'), may hold values from -0.0625 to 0.0625
- w_out: bfloat16 [8, 8, 1024, 7168], P('pipe', 'expert', 'dp'), may hold values from -0.1875 to 0.1875
Outputs:
- rising_out: bfloat16 [8, 2048, 7168], P('pipe', ('expert', 'dp'))
- sinking_out: bfloat16 [8, 2048, 7168], P('pipe', ('expert', 'dp'))
Inputs may be any that keep to these rules, and one draw needn't show every extreme that they name: `rising_ids`: each token names 2 different experts; in each device's aligned block of 128 tokens of a section no expert is named by more than 40 tokens, a bound that some block reaches. `sinking_ids`: each token names 2 different experts; in each device's aligned block of 128 tokens of a section no expert is named by more than 40 tokens, a bound that some block reaches. `rising_drop`: all 32 bits of each word are used. `sinking_drop`: all 32 bits of each word are used.
All inputs are finite; a program needn't handle non-finite values.
Results may differ from a plain program's by a relative error of at most 0.0072.
Values may be sent and summed in bfloat16 or wider, within the bound.
A program may use at most 128 MiB of HBM per device.

v0:
```python
import jax
import jax.numpy as jnp
from jax import lax
from jax.sharding import PartitionSpec as P

keep_scale = 1.0 / 0.9
root_half = 0.7071067811865476
inv_root_tau = 0.3989422804014327


def from_behind(block, axis, distance):
    devices = range(lax.axis_size(axis))
    route = [(i - distance, i) for i in devices if i - distance in devices]
    return lax.ppermute(block, axis, route)


def gelu_value(h):
    return h * (0.5 * (1.0 + lax.erf(h * root_half)))


def gelu_slope(h):
    return 0.5 * (1.0 + lax.erf(h * root_half)) + h * inv_root_tau * jnp.exp(-0.5 * h * h)


def unpack_keep(words):
    shifts = jnp.arange(32, dtype=jnp.int32)
    bits = jnp.right_shift(words[:, :, None], shifts[None, None, :]) & 1
    return bits.reshape(words.shape[0], words.shape[1] * 32).T.astype(jnp.float32)


def routing(ids, owners, cap):
    count = ids.shape[0]
    names = jnp.arange(owners, dtype=jnp.int32)
    named = ids[:, :, None] == names[None, None, :]
    hit = jnp.any(named, axis=1).astype(jnp.int32)
    place = jnp.cumsum(hit, axis=0) - 1
    seats = jnp.arange(cap, dtype=jnp.int32)
    match = (hit.T[:, None, :] == 1) & (place.T[:, None, :] == seats[None, :, None])
    tokens = jnp.arange(count, dtype=jnp.int32)
    filled = jnp.any(match, axis=2)
    token_of = jnp.sum(jnp.where(match, tokens[None, None, :], 0), axis=2) + jnp.where(
        filled, 0, count
    )
    return (token_of, place)


def pick_rows(values, token_of):
    padded = jnp.concatenate([values, jnp.zeros((1, values.shape[1]), values.dtype)], axis=0)
    return jnp.take(padded, token_of, axis=0)


def dispatch(send):
    owners, cap, width = send.shape
    pairs = lax.axis_size("dp")
    doubled = jnp.broadcast_to(send[:, None], (owners, pairs, cap, width)).reshape(
        owners * pairs, cap, width
    )
    arrived = lax.all_to_all(doubled, ("expert", "dp"), split_axis=0, concat_axis=0, tiled=True)
    return arrived.reshape(owners * pairs * cap, width)


def combine(parts, cap):
    slots, width = parts.shape
    pairs = lax.axis_size("dp")
    owners = slots // (pairs * cap)
    returned = lax.all_to_all(
        parts.reshape(owners * pairs, cap, width),
        ("expert", "dp"),
        split_axis=0,
        concat_axis=0,
        tiled=True,
    )
    summed = jnp.sum(returned.reshape(owners, pairs, cap, width).astype(jnp.float32), axis=1)
    return summed.astype(jnp.bfloat16)


def collect(results, ids, place, cap):
    width = results.shape[2]
    flat = results.reshape(-1, width)
    seat = jnp.take_along_axis(place, ids, axis=1)
    return jnp.take(flat, ids * cap + seat, axis=0).astype(jnp.float32)


def local(
    rising_in,
    rising_ids,
    rising_gates,
    rising_drop,
    sinking_grad,
    sinking_ids,
    sinking_gates,
    sinking_drop,
    sinking_pre,
    w_in,
    w_out,
):
    owners = lax.axis_size("expert")
    cap = sinking_pre.shape[2] // (owners * lax.axis_size("dp"))
    names = jnp.arange(owners, dtype=jnp.int32)
    inputs = rising_in[0]
    ids_one = rising_ids[0]
    coef_one = unpack_keep(rising_drop[0]) * rising_gates[0] * keep_scale
    token_one, place_one = routing(ids_one, owners, cap)
    received = dispatch(pick_rows(inputs, token_one))
    pre = jnp.dot(received, w_in[0, 0], preferred_element_type=jnp.float32)
    act = gelu_value(pre).astype(jnp.bfloat16)
    parts = jnp.dot(act, w_out[0, 0], preferred_element_type=jnp.float32).astype(jnp.bfloat16)
    expert_out = combine(parts, cap)
    gathered = collect(expert_out, ids_one, place_one, cap)
    forward = jnp.sum(coef_one[:, :, None] * gathered, axis=1).astype(jnp.bfloat16)
    ids_two = sinking_ids[0]
    coef_two = unpack_keep(sinking_drop[0]) * sinking_gates[0] * keep_scale
    token_two, place_two = routing(ids_two, owners, cap)
    weight = jnp.sum(
        jnp.where(ids_two[:, :, None] == names[None, None, :], coef_two[:, :, None], 0.0), axis=1
    )
    grad_f = sinking_grad[0].astype(jnp.float32)
    padded_weight = jnp.concatenate([weight, jnp.zeros((1, owners), jnp.float32)], axis=0)
    seat_weight = jnp.take(padded_weight, token_two, axis=0)
    picked = pick_rows(grad_f, token_two)
    own_weight = jnp.take_along_axis(seat_weight, names[:, None, None], axis=2)
    send = (own_weight * picked).astype(jnp.bfloat16)
    arrived = dispatch(send)
    back_act = lax.dot_general(
        arrived, w_out[0, 0], (((1,), (1,)), ((), ())), preferred_element_type=jnp.float32
    )
    back_pre = (back_act * gelu_slope(sinking_pre[0, 0].astype(jnp.float32))).astype(jnp.bfloat16)
    grad_parts = lax.dot_general(
        back_pre, w_in[0, 0], (((1,), (1,)), ((), ())), preferred_element_type=jnp.float32
    ).astype(jnp.bfloat16)
    expert_grad = combine(grad_parts, cap)
    backward = jnp.sum(collect(expert_grad, ids_two, place_two, cap), axis=1).astype(jnp.bfloat16)
    handed_forward, handed_backward = from_behind((forward[None], backward[None]), "pipe", 1)
    return (handed_forward, handed_backward)


def solution(mesh):
    placed = (
        P("pipe", ("expert", "dp"), None),
        P("pipe", ("expert", "dp"), None),
        P("pipe", ("expert", "dp"), None),
        P("pipe", None, ("expert", "dp")),
        P("pipe", ("expert", "dp"), None),
        P("pipe", ("expert", "dp"), None),
        P("pipe", ("expert", "dp"), None),
        P("pipe", None, ("expert", "dp")),
        P("pipe", "expert", None, "dp"),
        P("pipe", "expert", None, "dp"),
        P("pipe", "expert", "dp", None),
    )
    return jax.shard_map(
        local,
        mesh=mesh,
        in_specs=placed,
        out_specs=(P("pipe", ("expert", "dp"), None), P("pipe", ("expert", "dp"), None)),
        check_vma=False,
    )
```

profile of v0, /device:TPU:24, one launch (start us, length us, event | category | flops | bytes accessed | tf_op | source)
XLA Modules:
  0.0 652.5 jit_solution(11412043962344546521)
XLA Ops:
  0.6 0.7 fusion.26
  1.3 0.1 copy.45
  1.4 0.2 reduce_window_sum.17
  1.7 0.2 select_reduce_fusion.1
  1.9 0.2 fusion.22
  2.2 1.7 concatenate.11
  3.9 6.2 gather_fusion
  10.1 4.9 broadcast_select_fusion.2
  15.0 7.0 %broadcast_in_dim.133 = bf16[8,2,40,7168]{3,2,1,0:T(8,128)(2,1)} broadcast(bf16[8,40,7168]{2,1,0:T(8,128)(2,1)} %broadcast_select_fusion.2), dimensions={0,2,3} | broadcast | bytes 13762560 | tf_op jit(solution)/shard_map/broadcast_in_dim | solution.py:55
  22.0 8.1 %all-to-all-start = ((bf16[16,40,7168]{2,1,0:T(8,128)(2,1)}), bf16[16,40,7168]{2,1,0:T(8,128)(2,1)}, u32[]{:S(2)}, u32[]{:S(2)}) async-start(bf16[16,40,7168]{2,1,0:T(8,128)(2,1)} %bitcast.96), calls=%async_computation | async-start | bytes 18350080 | tf_op jit(solution)/shard_map/all_to_all | solution.py:58
  30.2 0.1 shift_right_arithmetic.53
  30.3 0.1 shift_right_arithmetic.48
  30.4 0.1 shift_right_arithmetic.46
  30.5 0.1 copy.51
  30.6 0.2 reduce_window_sum.18
  30.9 0.2 fusion.24
  31.1 0.2 select_reduce_fusion
  31.4 0.1 reshape.225
  31.5 0.1 copy.56
  31.6 2.4 pad_convert_fusion
  34.0 14.6 %gather_fusion.2 = f32[320,7168]{1,0:T(8,128)} fusion(f32[129,7168]{1,0:T(8,128)} %pad_convert_fusion, s32[1024]{0:T(1024)S(1)} %pad_clamp_fusion.1), kind=kCustom, calls=%fused_computation.6 | custom fusion | bytes 18351360 | tf_op jit(solution)/shard_map/jit(_take)/gather | solution.py:49
  48.6 1.1 gather_fusion.1
  49.9 0.6 gather_fusion.3
  50.5 7.4 %multiply_convert_fusion = bf16[8,40,7168]{2,1,0:T(8,128)(2,1)} fusion(f32[8,40,7168]{2,1,0:T(8,128)} %bitcast.98, f32[8,40]{1,0:T(8,128)S(1)} %broadcast_select_fusion.4, pred[8,40]{1,0:T(8,128)(4,1)S(1)} %compare_and_fusion), kind=kLoop, calls=%fused_computation.12 | loop fusion | flops 6881280 | bytes 13764160 | tf_op jit(solution)/shard_map/convert_element_type | solution.py:122
  58.0 95.6 %all-to-all-done = bf16[16,40,7168]{2,1,0:T(8,128)(2,1)} async-done(((bf16[16,40,7168]{2,1,0:T(8,128)(2,1)}), bf16[16,40,7168]{2,1,0:T(8,128)(2,1)}, u32[]{:S(2)}, u32[]{:S(2)}) %all-to-all-start) | async-done | bytes 9175072 | tf_op jit(solution)/shard_map/all_to_all | solution.py:58
  153.6 7.0 %broadcast_in_dim.143 = bf16[8,2,40,7168]{3,2,1,0:T(8,128)(2,1)} broadcast(bf16[8,40,7168]{2,1,0:T(8,128)(2,1)} %multiply_convert_fusion), dimensions={0,2,3} | broadcast | bytes 13762560 | tf_op jit(solution)/shard_map/broadcast_in_dim | solution.py:55
  160.6 6.3 all-to-all-start.2
  166.9 10.7 %multiply_convert_fusion.1 = bf16[640,512]{1,0:T(8,128)(2,1)S(1)} fusion(bf16[640,7168]{1,0:T(8,128)(2,1)} %bitcast.11, bf16[1,1,7168,512]{3,2,1,0:T(8,128)(2,1)} %param.24), kind=kOutput, calls=%fused_computation.38 | convolution fusion | flops 4699258880 | bytes 17170432 | tf_op jit(solution)/shard_map/dot_general | solution.py:105
  177.6 10.4 %convolution_convert_fusion.1 = bf16[640,7168]{1,0:T(8,128)(2,1)} fusion(bf16[640,512]{1,0:T(8,128)(2,1)S(1)} %multiply_convert_fusion.1, bf16[1,1,512,7168]{3,2,1,0:T(8,128)(2,1)} %param.25), kind=kOutput, calls=%fused_computation.9 | convolution fusion | flops 4702208000 | bytes 17170432 | tf_op jit(solution)/shard_map/dot_general | solution.py:107
  188.0 102.5 %all-to-all-done.2 = bf16[16,40,7168]{2,1,0:T(8,128)(2,1)} async-done(((bf16[16,40,7168]{2,1,0:T(8,128)(2,1)}), bf16[16,40,7168]{2,1,0:T(8,128)(2,1)}, u32[]{:S(2)}, u32[]{:S(2)}) %all-to-all-start.2) | async-done | bytes 9175072 | tf_op jit(solution)/shard_map/all_to_all | solution.py:58
  290.5 6.2 all-to-all-start.1
  296.7 10.9 %fusion.10 = bf16[640,512]{1,0:T(8,128)(2,1)S(1)} fusion(bf16[640,7168]{1,0:T(8,128)(2,1)} %bitcast.32, bf16[1,1,512,7168]{3,2,1,0:T(8,128)(2,1)} %param.25, bf16[1,1,640,512]{3,2,1,0:T(8,128)(2,1)S(1)} %copy-done.7), kind=kOutput, calls=%fused_computation.31 | convolution fusion | flops 4701224960 | bytes 17825792 | tf_op jit(solution)/shard_map/dot_general | solution.py:124
  307.6 10.3 %convolution_convert_fusion = bf16[640,7168]{1,0:T(8,128)(2,1)} fusion(bf16[640,512]{1,0:T(8,128)(2,1)S(1)} %fusion.10, bf16[1,1,7168,512]{3,2,1,0:T(8,128)(2,1)} %param.24), kind=kOutput, calls=%fused_computation.8 | convolution fusion | flops 4702208000 | bytes 17170432 | tf_op jit(solution)/shard_map/dot_general | solution.py:128
  318.0 102.2 %all-to-all-done.1 = bf16[16,40,7168]{2,1,0:T(8,128)(2,1)} async-done(((bf16[16,40,7168]{2,1,0:T(8,128)(2,1)}), bf16[16,40,7168]{2,1,0:T(8,128)(2,1)}, u32[]{:S(2)}, u32[]{:S(2)}) %all-to-all-start.1) | async-done | bytes 9175072 | tf_op jit(solution)/shard_map/all_to_all | solution.py:66
  420.2 6.5 all-to-all-start.3
  426.7 0.1 copy.46
  426.9 0.1 reshape.266
  427.0 1.9 gather_fusion.4
  429.0 0.1 reshape.269
  429.2 0.1 copy.50
  429.3 0.1 reshape.270
  429.5 0.1 copy.48
  429.6 0.1 copy.44
  429.7 0.1 copy.52
  429.8 0.1 reshape.275
  430.0 1.9 gather_fusion.6
  431.9 0.1 reshape.278
  432.2 0.1 copy.58
  432.3 0.1 reshape.279
  432.4 0.1 copy.54
  432.6 9.1 %bitcast_reduce_fusion.1 = bf16[8,40,7168]{2,1,0:T(8,128)(2,1)} fusion(bf16[16,40,7168]{2,1,0:T(8,128)(2,1)} %all-to-all-done.1), kind=kLoop, calls=%fused_computation.11 | loop fusion | flops 2293760 | bytes 13762560 | tf_op jit(solution)/shard_map/reduce_sum | solution.py:73
  441.6 10.9 %gather_fusion.5 = bf16[256,7168]{1,0:T(8,128)(2,1)} fusion(bf16[320,7168]{1,0:T(8,128)(2,1)} %bitcast.94, s32[1024]{0:T(1024)S(1)} %pad_clamp_fusion.2), kind=kCustom, calls=%fused_computation.1.clone | custom fusion | bytes 7341056 | tf_op jit(solution)/shard_map/jit(_take)/gather | solution.py:81
  452.6 8.3 %reshape.273 = bf16[128,2,7168]{2,1,0:T(2,128)(2,1)} reshape(bf16[256,7168]{1,0:T(8,128)(2,1)} %gather_fusion.5) | data formatting | bytes 7340032 | tf_op jit(solution)/shard_map/jit(_take)/gather | solution.py:81
  460.8 14.0 %multiply_reduce_fusion = bf16[128,7168]{1,0:T(8,128)(2,1)} fusion(bf16[128,2,7168]{2,1,0:T(2,128)(2,1)} %reshape.273, pred[128,2]{1,0:T(8,128)(4,1)S(1)} %copy.48, f32[128,2]{1,0:T(8,128)S(1)} %copy.44), kind=kLoop, calls=%fused_computation.19 | loop fusion | flops 6422528 | bytes 5506304 | tf_op jit(solution)/shard_map/reduce_sum | solution.py:110
  474.8 2.9 collective-permute-start
  477.7 72.5 %all-to-all-done.3 = bf16[16,40,7168]{2,1,0:T(8,128)(2,1)} async-done(((bf16[16,40,7168]{2,1,0:T(8,128)(2,1)}), bf16[16,40,7168]{2,1,0:T(8,128)(2,1)}, u32[]{:S(2)}, u32[]{:S(2)}) %all-to-all-start.3) | async-done | bytes 9175072 | tf_op jit(solution)/shard_map/all_to_all | solution.py:66
  550.2 9.1 %bitcast_reduce_fusion = bf16[8,40,7168]{2,1,0:T(8,128)(2,1)} fusion(bf16[16,40,7168]{2,1,0:T(8,128)(2,1)} %all-to-all-done.3), kind=kLoop, calls=%fused_computation.10 | loop fusion | flops 2293760 | bytes 13762560 | tf_op jit(solution)/shard_map/reduce_sum | solution.py:73
  559.3 10.9 %gather_fusion.7 = bf16[256,7168]{1,0:T(8,128)(2,1)} fusion(bf16[320,7168]{1,0:T(8,128)(2,1)} %bitcast.95, s32[1024]{0:T(1024)S(1)} %pad_clamp_fusion), kind=kCustom, calls=%fused_computation.3.clone | custom fusion | bytes 7341056 | tf_op jit(solution)/shard_map/jit(_take)/gather | solution.py:81
  570.2 8.3 %reshape.282 = bf16[128,2,7168]{2,1,0:T(2,128)(2,1)} reshape(bf16[256,7168]{1,0:T(8,128)(2,1)} %gather_fusion.7) | data formatting | bytes 7340032 | tf_op jit(solution)/shard_map/jit(_take)/gather | solution.py:81
  578.5 9.4 %fusion.6 = bf16[128,7168]{1,0:T(8,128)(2,1)S(1)} fusion(bf16[128,2,7168]{2,1,0:T(2,128)(2,1)} %reshape.282, pred[128,2]{1,0:T(8,128)(4,1)S(1)} %copy.54), kind=kLoop, calls=%fused_computation.23 | loop fusion | flops 2752512 | bytes 5505280 | tf_op jit(solution)/shard_map/reduce_sum | solution.py:132
  588.0 21.3 %collective-permute-start.1 = (bf16[1,128,7168]{2,1,0:T(8,128)(2,1)S(1)}, bf16[1,128,7168]{2,1,0:T(8,128)(2,1)S(1)}, u32[]{:S(2)}, u32[]{:S(2)}) collective-permute-start(bf16[1,128,7168]{2,1,0:T(8,128)(2,1)S(1)} %bitcast.104), channel_id=1, source_target_pairs={{0,16},{16,32},{32,48},{48,64},{64,80},{80,96},{96,112},{1,17},{17... | collective-permute-start | bytes 5505032 | tf_op jit(solution)/shard_map/ppermute | solution.py:14
  609.2 40.6 %collective-permute-done.1 = bf16[1,128,7168]{2,1,0:T(8,128)(2,1)S(1)} collective-permute-done((bf16[1,128,7168]{2,1,0:T(8,128)(2,1)S(1)}, bf16[1,128,7168]{2,1,0:T(8,128)(2,1)S(1)}, u32[]{:S(2)}, u32[]{:S(2)}) %collective-permute-start.1) | collective-permute-done | bytes 1835040 | tf_op jit(solution)/shard_map/ppermute | solution.py:14
  649.9 1.2 copy.61
  651.1 1.2 copy.62
  (52 shorter events, 0.9 us)
Async XLA Ops:
  22.0 8.1 %copy-start.3 = (s32[1,2,4]{2,1,0:T(2,128)S(1)}, s32[1,2,4]{2,1,0:T(2,128)}, u32[]{:S(2)}) copy-start(s32[1,2,4]{2,1,0:T(2,128)} %param.22) | copy-start | bytes 100
  22.0 8.4 %copy-start.4 = (s32[1,2,4]{2,1,0:T(2,128)S(1)}, s32[1,2,4]{2,1,0:T(2,128)}, u32[]{:S(2)}) copy-start(s32[1,2,4]{2,1,0:T(2,128)} %param.18) | copy-start | bytes 100
  22.0 8.5 %copy-start.1 = (s32[1,128,2]{1,2,0:T(2,128)S(1)}, s32[1,128,2]{1,2,0:T(2,128)}, u32[]{:S(2)}) copy-start(s32[1,128,2]{1,2,0:T(2,128)} %param.20) | copy-start | bytes 3076
  22.0 9.5 %copy-start.5 = (f32[1,128,2]{1,2,0:T(2,128)S(1)}, f32[1,128,2]{1,2,0:T(2,128)}, u32[]{:S(2)}) copy-start(f32[1,128,2]{1,2,0:T(2,128)} %param.21) | copy-start | bytes 3076
  22.0 9.5 %copy-start.6 = (f32[1,128,2]{1,2,0:T(2,128)S(1)}, f32[1,128,2]{1,2,0:T(2,128)}, u32[]{:S(2)}) copy-start(f32[1,128,2]{1,2,0:T(2,128)} %param.17) | copy-start | bytes 3076
  22.0 9.6 %copy-start = (bf16[1,128,7168]{2,1,0:T(8,128)(2,1)S(1)}, bf16[1,128,7168]{2,1,0:T(8,128)(2,1)}, u32[]{:S(2)}) copy-start(bf16[1,128,7168]{2,1,0:T(8,128)(2,1)} %param.19) | copy-start | bytes 5505028
  22.0 131.6 %all-to-all-start = ((bf16[16,40,7168]{2,1,0:T(8,128)(2,1)}), bf16[16,40,7168]{2,1,0:T(8,128)(2,1)}, u32[]{:S(2)}, u32[]{:S(2)}) async-start(bf16[16,40,7168]{2,1,0:T(8,128)(2,1)} %bitcast.96), calls=%async_computation | async-start | bytes 18350080 | tf_op jit(solution)/shard_map/all_to_all | solution.py:58
  160.6 129.8 %all-to-all-start.2 = ((bf16[16,40,7168]{2,1,0:T(8,128)(2,1)}), bf16[16,40,7168]{2,1,0:T(8,128)(2,1)}, u32[]{:S(2)}, u32[]{:S(2)}) async-start(bf16[16,40,7168]{2,1,0:T(8,128)(2,1)} %bitcast.97), calls=%async_computation.2 | async-start | bytes 18350080 | tf_op jit(solution)/shard_map/all_to_all | solution.py:58
  290.5 6.2 copy-start.7
  290.5 129.7 %all-to-all-start.1 = ((bf16[16,40,7168]{2,1,0:T(8,128)(2,1)}), bf16[16,40,7168]{2,1,0:T(8,128)(2,1)}, u32[]{:S(2)}, u32[]{:S(2)}) async-start(bf16[16,40,7168]{2,1,0:T(8,128)(2,1)} %bitcast.101), calls=%async_computation.1 | async-start | bytes 18350080 | tf_op jit(solution)/shard_map/all_to_all | solution.py:66
  420.2 6.5 %copy-start.2 = (s32[1,128,2]{1,2,0:T(2,128)S(1)}, s32[1,128,2]{1,2,0:T(2,128)}, u32[]{:S(2)}) copy-start(s32[1,128,2]{1,2,0:T(2,128)} %param.16) | copy-start | bytes 3076
  420.2 130.1 %all-to-all-start.3 = ((bf16[16,40,7168]{2,1,0:T(8,128)(2,1)}), bf16[16,40,7168]{2,1,0:T(8,128)(2,1)}, u32[]{:S(2)}, u32[]{:S(2)}) async-start(bf16[16,40,7168]{2,1,0:T(8,128)(2,1)} %bitcast.100), calls=%async_computation.3 | async-start | bytes 18350080 | tf_op jit(solution)/shard_map/all_to_all | solution.py:66
  474.8 134.4 %collective-permute-start = (bf16[1,128,7168]{2,1,0:T(8,128)(2,1)}, bf16[1,128,7168]{2,1,0:T(8,128)(2,1)S(1)}, u32[]{:S(2)}, u32[]{:S(2)}) collective-permute-start(bf16[1,128,7168]{2,1,0:T(8,128)(2,1)} %bitcast.87), channel_id=1, source_target_pairs={{0,16},{16,32},{32,48},{48,64},{64,80},{80,96},{96,112},{1,17},{17... | collective-permute-start | bytes 5505032 | tf_op jit(solution)/shard_map/ppermute | solution.py:14
  588.0 61.9 %collective-permute-start.1 = (bf16[1,128,7168]{2,1,0:T(8,128)(2,1)S(1)}, bf16[1,128,7168]{2,1,0:T(8,128)(2,1)S(1)}, u32[]{:S(2)}, u32[]{:S(2)}) collective-permute-start(bf16[1,128,7168]{2,1,0:T(8,128)(2,1)S(1)} %bitcast.104), channel_id=1, source_target_pairs={{0,16},{16,32},{32,48},{48,64},{64,80},{80,96},{96,112},{1,17},{17... | collective-permute-start | bytes 5505032 | tf_op jit(solution)/shard_map/ppermute | solution.py:14
where the time goes:
time: 658 us; the launch traced here: 653 us
  waiting for transfers between devices  414 us (63%)
  local copies, waits for them, and re-layouts  85.8 us (13%)
  other arithmetic  58.4 us (9%)
  starting transfers between devices  51.3 us (8%)
  matrix products  42.3 us (6%)
    all_to_all x2, waiting for transfers between devices, dispatch(): lax.all_to_all(doubled, ('expert', 'dp'), split_axis=0, concat_axis=0, ti...  198 us
    all_to_all x2, waiting for transfers between devices, combine(): lax.all_to_all(parts.reshape(owners * pairs, cap, width), ('expert', 'dp'...  175 us
    ppermute x2, waiting for transfers between devices, from_behind(): return lax.ppermute(block, axis, route)  40.6 us
    gather x4, local copies, waits for them, and re-layouts, collect(): return jnp.take(flat, ids * cap + seat, axis=0).astype(jnp.float32)  38.4 us
    ppermute x2, starting transfers between devices, from_behind(): return lax.ppermute(block, axis, route)  24.2 us
    gather x2, local copies, waits for them, and re-layouts, pick_rows(): return jnp.take(padded, token_of, axis=0)  20.9 us
    reduce_sum x2, other arithmetic, combine(): jnp.sum(returned.reshape(owners, pairs, cap, width).astype(jnp.float32),...  18.1 us
    all_to_all x2, starting transfers between devices, dispatch(): lax.all_to_all(doubled, ('expert', 'dp'), split_axis=0, concat_axis=0, ti...  14.4 us
  transfers between devices with their start and end apart: 6, of which 5 were waited for; matrix products, arithmetic and copies ran while one was open for 24% of the time, Pallas kernels for 0%

commit v1 on v0

v1 whole, which is shorter than its diff:
```python
import jax
import jax.numpy as jnp
from jax import lax
from jax.sharding import PartitionSpec as P

keep_scale = 1.0 / 0.9
root_half = 0.7071067811865476
inv_root_tau = 0.3989422804014327


def from_behind(block, axis, distance):
    devices = range(lax.axis_size(axis))
    route = [(i - distance, i) for i in devices if i - distance in devices]
    return lax.ppermute(block, axis, route)


def swap_cores(block):
    return lax.ppermute(block, "dp", [(0, 1), (1, 0)])


def gelu_value(h):
    return h * (0.5 * (1.0 + lax.erf(h * root_half)))


def gelu_slope(h):
    return 0.5 * (1.0 + lax.erf(h * root_half)) + h * inv_root_tau * jnp.exp(-0.5 * h * h)


def unpack_keep(words):
    shifts = jnp.arange(32, dtype=jnp.int32)
    bits = jnp.right_shift(words[:, :, None], shifts[None, None, :]) & 1
    return bits.reshape(words.shape[0], words.shape[1] * 32).T.astype(jnp.float32)


def routing(ids, owners, cap):
    count = ids.shape[0]
    names = jnp.arange(owners, dtype=jnp.int32)
    named = ids[:, :, None] == names[None, None, :]
    hit = jnp.any(named, axis=1).astype(jnp.int32)
    place = jnp.cumsum(hit, axis=0) - 1
    seat = jnp.sum(jnp.where(named, place[:, None, :], 0), axis=2)
    return ids * cap + seat


def pick(slots, rows):
    seats = jnp.arange(rows, dtype=jnp.int32)
    return [(slots[:, k : k + 1] == seats[None, :]) for k in range(slots.shape[1])]


def spread(hot, values):
    return lax.dot_general(
        hot.astype(jnp.bfloat16), values, (((0,), (0,)), ((), ())), preferred_element_type=jnp.float32
    )


def dispatch(send):
    own = lax.all_to_all(send, "expert", split_axis=0, concat_axis=0, tiled=True)
    own = own.reshape(-1, own.shape[2])
    return own, swap_cores(own)


def combine(own, other, owners):
    added = own.astype(jnp.float32) + swap_cores(other).astype(jnp.float32)
    added = added.astype(jnp.bfloat16).reshape(owners, -1, own.shape[1])
    back = lax.all_to_all(added, "expert", split_axis=0, concat_axis=0, tiled=True)
    return back.reshape(-1, own.shape[1])


def local(
    rising_in,
    rising_ids,
    rising_gates,
    rising_drop,
    sinking_grad,
    sinking_ids,
    sinking_gates,
    sinking_drop,
    sinking_pre,
    w_in,
    w_out,
):
    owners = lax.axis_size("expert")
    pairs = lax.axis_size("dp")
    me = lax.axis_index("dp")
    slots = sinking_pre.shape[2]
    cap = slots // (owners * pairs)
    rows = owners * cap
    wi, wo = w_in[0, 0], w_out[0, 0]
    coef_one = unpack_keep(rising_drop[0]) * rising_gates[0] * keep_scale
    coef_two = unpack_keep(sinking_drop[0]) * sinking_gates[0] * keep_scale
    hot_one = pick(routing(rising_ids[0], owners, cap), rows)
    hot_two = pick(routing(sinking_ids[0], owners, cap), rows)

    send_one = spread(hot_one[0] | hot_one[1], rising_in[0]).astype(jnp.bfloat16)
    weight = jnp.sum(
        sum(jnp.where(hot_two[k], coef_two[:, k : k + 1], 0.0) for k in range(2)), axis=0
    )
    send_two = (weight[:, None] * spread(hot_two[0] | hot_two[1], sinking_grad[0])).astype(jnp.bfloat16)

    got_one = dispatch(send_one.reshape(owners, cap, -1))
    got_two = dispatch(send_two.reshape(owners, cap, -1))

    def forward_part(got):
        act = gelu_value(jnp.dot(got, wi, preferred_element_type=jnp.float32)).astype(jnp.bfloat16)
        return jnp.dot(act, wo, preferred_element_type=jnp.float32).astype(jnp.bfloat16)

    pre = sinking_pre[0, 0].reshape(owners, pairs, cap, -1)

    def backward_part(got, core):
        saved = lax.dynamic_index_in_dim(pre, core, 1, keepdims=False).reshape(rows, -1)
        act = lax.dot_general(got, wo, (((1,), (1,)), ((), ())), preferred_element_type=jnp.float32)
        mid = (act * gelu_slope(saved.astype(jnp.float32))).astype(jnp.bfloat16)
        return lax.dot_general(
            mid, wi, (((1,), (1,)), ((), ())), preferred_element_type=jnp.float32
        ).astype(jnp.bfloat16)

    back_one = combine(forward_part(got_one[0]), forward_part(got_one[1]), owners)
    back_two = combine(backward_part(got_two[0], me), backward_part(got_two[1], 1 - me), owners)

    def collect(hot, back):
        return jnp.dot(hot.astype(jnp.bfloat16), back, preferred_element_type=jnp.float32)

    forward = sum(coef_one[:, k : k + 1] * collect(hot_one[k], back_one) for k in range(2))
    handed_forward = from_behind(forward.astype(jnp.bfloat16)[None], "pipe", 1)
    backward = collect(hot_two[0] | hot_two[1], back_two)
    handed_backward = from_behind(backward.astype(jnp.bfloat16)[None], "pipe", 1)
    return (handed_forward, handed_backward)


def solution(mesh):
    placed = (
        P("pipe", ("expert", "dp"), None),
        P("pipe", ("expert", "dp"), None),
        P("pipe", ("expert", "dp"), None),
        P("pipe", None, ("expert", "dp")),
        P("pipe", ("expert", "dp"), None),
        P("pipe", ("expert", "dp"), None),
        P("pipe", ("expert", "dp"), None),
        P("pipe", None, ("expert", "dp")),
        P("pipe", "expert", None, "dp"),
        P("pipe", "expert", None, "dp"),
        P("pipe", "expert", "dp", None),
    )
    return jax.shard_map(
        local,
        mesh=mesh,
        in_specs=placed,
        out_specs=(P("pipe", ("expert", "dp"), None), P("pipe", ("expert", "dp"), None)),
        check_vma=False,
    )
```

time: 658 us -> 448 us (0.68)
  the two profiles are of different devices: /device:TPU:24 before, /device:TPU:20 now
where the time goes in v1:
time: 448 us; the launch traced here: 447 us
  waiting for transfers between devices  228 us (51%)
  matrix products  70.7 us (16%)
  starting transfers between devices  70.1 us (16%)
  blocking collectives  69.1 us (15%)
  local copies, waits for them, and re-layouts  4.9 us (1%)
    all_to_all x2, waiting for transfers between devices, combine(): lax.all_to_all(added, 'expert', split_axis=0, concat_axis=0, tiled=True)  91.7 us
    ppermute x2, waiting for transfers between devices, from_behind(): return lax.ppermute(block, axis, route)  79.4 us
    all_to_all x1, blocking collectives, dispatch(): lax.all_to_all(send, 'expert', split_axis=0, concat_axis=0, tiled=True)  69.1 us
    all_to_all x1, waiting for transfers between devices, dispatch(): lax.all_to_all(send, 'expert', split_axis=0, concat_axis=0, tiled=True)  57.3 us
    ppermute x2, starting transfers between devices, from_behind(): return lax.ppermute(block, axis, route)  39.7 us
    all_to_all x2, starting transfers between devices, combine(): lax.all_to_all(added, 'expert', split_axis=0, concat_axis=0, tiled=True)  21.6 us
    dot_general x2, matrix products, forward_part(): jnp.dot(act, wo, preferred_element_type=jnp.float32).astype(jnp.bfloat16)  20.7 us
    dot_general x2, matrix products, backward_part(): lax.dot_general(got, wo, (((1,), (1,)), ((), ())), preferred_element_type...  14.5 us
  transfers between devices with their start and end apart: 9, of which 4 were waited for; matrix products, arithmetic and copies ran while one was open for 15% of the time, Pallas kernels for 0%

profile of v1, /device:TPU:20, one launch (start us, length us, event | category | flops | bytes accessed | tf_op | source)
XLA Modules:
  0.0 446.9 jit_solution(2737848762785902993)
XLA Ops:
  0.6 0.0 copy-start
  0.6 0.8 fusion.72
  1.5 0.1 copy.17
  1.6 0.2 reduce_window_sum.17
  1.8 0.7 select_reduce_fusion.1
  2.5 0.7 multiply_add_fusion.1
  3.2 0.0 copy-done
  3.2 3.6 convolution_convert_fusion.4
  6.8 0.0 copy-start.8
  6.8 0.0 copy-start.2
  6.8 8.3 %all-to-all-start = ((bf16[8,40,7168]{2,1,0:T(8,128)(2,1)}), bf16[8,40,7168]{2,1,0:T(8,128)(2,1)}, u32[]{:S(2)}, u32[]{:S(2)}) async-start(bf16[8,40,7168]{2,1,0:T(8,128)(2,1)} %bitcast.109), calls=%async_computation | async-start | bytes 9175040 | tf_op jit(solution)/shard_map/all_to_all | solution.py:57
  15.1 0.1 shift_right_arithmetic.48
  15.2 0.0 copy-done.4
  15.2 0.0 copy-done.5
  15.2 0.1 shift_right_arithmetic.45
  15.3 0.1 shift_right_arithmetic.46
  15.3 0.0 copy-done.6
  15.3 0.1 shift_right_arithmetic.52
  15.4 0.1 shift_right_arithmetic.53
  15.5 0.1 copy.19
  15.6 0.2 reduce_window_sum.18
  15.9 0.0 copy-done.7
  15.9 0.0 copy-done.8
  15.9 57.3 %all-to-all-done = bf16[8,40,7168]{2,1,0:T(8,128)(2,1)} async-done(((bf16[8,40,7168]{2,1,0:T(8,128)(2,1)}), bf16[8,40,7168]{2,1,0:T(8,128)(2,1)}, u32[]{:S(2)}, u32[]{:S(2)}) %all-to-all-start) | async-done | bytes 4587552 | tf_op jit(solution)/shard_map/all_to_all | solution.py:57
  73.2 0.0 collective-permute-start
  73.2 0.1 add_reduce_fusion
  73.4 0.0 copy-done.2
  73.4 1.3 fusion
  74.7 69.1 %all_to_all.20 = bf16[8,40,7168]{2,1,0:T(8,128)(2,1)} all-to-all(bf16[8,40,7168]{2,1,0:T(8,128)(2,1)S(1)} %bitcast.110), channel_id=1, replica_groups=mesh['pipe'=8,'expert'=8,'dp'=2] {'expert'}, dimensions={0} | all-to-all | bytes 9175040 | tf_op jit(solution)/shard_map/all_to_all | solution.py:57
  143.8 0.0 collective-permute-start.3
  143.8 0.0 collective-permute-done
  143.8 13.7 %convolution_convert_fusion.2 = bf16[320,7168]{1,0:T(8,128)(2,1)} fusion(bf16[1,1,512,7168]{3,2,1,0:T(8,128)(2,1)} %param.21, bf16[320,7168]{1,0:T(8,128)(2,1)} %collective-permute-done, bf16[1,1,7168,512]{3,2,1,0:T(8,128)(2,1)} %param.20), kind=kOutput, calls=%fused_computation.5 | convolution fusion | flops 4700733440 | bytes 23855104 | tf_op jit(solution)/shard_map/dot_general | solution.py:105
  157.5 0.4 collective-permute-start.1
  158.0 0.0 copy-done.3
  158.0 0.0 collective-permute-done.3
  158.1 0.0 slice-start.1
  158.1 7.3 %fusion.31 = bf16[320,512]{1,0:T(8,128)(2,1)S(1)} fusion(bf16[320,7168]{1,0:T(8,128)(2,1)} %collective-permute-done.3, bf16[1,1,512,7168]{3,2,1,0:T(8,128)(2,1)} %param.21, bf16[320,512]{1,0:T(8,128)(2,1)S(1)} %bitcast.117), kind=kOutput, calls=%fused_computation.34 | convolution fusion | flops 2350612480 | bytes 12582912 | tf_op jit(solution)/shard_map/dot_general | solution.py:111
  165.4 0.0 slice-done
  165.4 0.0 slice-done.1
  165.4 0.0 slice-start.2
  165.4 4.7 %convolution_convert_fusion = bf16[320,7168]{1,0:T(8,128)(2,1)} fusion(bf16[320,512]{1,0:T(8,128)(2,1)S(1)} %fusion.31, bf16[1,1,7168,512]{3,2,1,0:T(8,128)(2,1)S(1)} %bitcast.108), kind=kOutput, calls=%fused_computation.2 | convolution fusion | flops 2351104000 | bytes 12255232 | tf_op jit(solution)/shard_map/dot_general | solution.py:113
  170.1 0.1 collective-permute-start.4
  170.1 5.0 %multiply_convert_fusion.1 = bf16[320,512]{1,0:T(8,128)(2,1)S(1)} fusion(bf16[320,7168]{1,0:T(8,128)(2,1)} %bitcast.9, bf16[1,1,7168,512]{3,2,1,0:T(8,128)(2,1)S(1)} %bitcast.108), kind=kOutput, calls=%fused_computation.57 | convolution fusion | flops 2349629440 | bytes 12255232 | tf_op jit(solution)/shard_map/dot_general | solution.py:104
  175.2 0.0 collective-permute-done.1
  175.2 0.0 slice-done.2
  175.2 0.0 slice-done.3
  175.2 7.0 %add_convert_fusion.1 = bf16[320,7168]{1,0:T(8,128)(2,1)} fusion(bf16[320,7168]{1,0:T(8,128)(2,1)} %collective-permute-done.1, bf16[320,512]{1,0:T(8,128)(2,1)S(1)} %multiply_convert_fusion.1, bf16[1,1,512,7168]{3,2,1,0:T(8,128)(2,1)S(1)} %bitcast.112), kind=kOutput, calls=%fused_computation.10 | convolution fusion | flops 2360279040 | bytes 16842752 | tf_op jit(solution)/shard_map/dot_general | solution.py:105
  182.2 6.9 %all-to-all-start.1 = ((bf16[8,40,7168]{2,1,0:T(8,128)(2,1)}), bf16[8,40,7168]{2,1,0:T(8,128)(2,1)}, u32[]{:S(2)}, u32[]{:S(2)}) async-start(bf16[8,40,7168]{2,1,0:T(8,128)(2,1)} %bitcast.114), calls=%async_computation.1 | async-start | bytes 9175040 | tf_op jit(solution)/shard_map/all_to_all | solution.py:65
  189.1 7.2 %fusion.34 = bf16[320,512]{1,0:T(8,128)(2,1)S(1)} fusion(bf16[320,7168]{1,0:T(8,128)(2,1)} %bitcast.26, bf16[1,1,512,7168]{3,2,1,0:T(8,128)(2,1)} %param.21, bf16[320,512]{1,0:T(8,128)(2,1)S(1)} %bitcast.116), kind=kOutput, calls=%fused_computation.35 | convolution fusion | flops 2350612480 | bytes 12582912 | tf_op jit(solution)/shard_map/dot_general | solution.py:111
  196.3 0.0 collective-permute-done.4
  196.3 9.1 %add_convert_fusion = bf16[320,7168]{1,0:T(8,128)(2,1)} fusion(bf16[320,7168]{1,0:T(8,128)(2,1)} %collective-permute-done.4, bf16[320,512]{1,0:T(8,128)(2,1)S(1)} %fusion.34, bf16[1,1,7168,512]{3,2,1,0:T(8,128)(2,1)} %param.20), kind=kOutput, calls=%fused_computation.9 | convolution fusion | flops 2360279040 | bytes 16842752 | tf_op jit(solution)/shard_map/dot_general | solution.py:113
  205.3 45.1 %all-to-all-done.1 = bf16[8,40,7168]{2,1,0:T(8,128)(2,1)} async-done(((bf16[8,40,7168]{2,1,0:T(8,128)(2,1)}), bf16[8,40,7168]{2,1,0:T(8,128)(2,1)}, u32[]{:S(2)}, u32[]{:S(2)}) %all-to-all-start.1) | async-done | bytes 4587552 | tf_op jit(solution)/shard_map/all_to_all | solution.py:65
  250.4 14.7 %all-to-all-start.3 = ((bf16[8,40,7168]{2,1,0:T(8,128)(2,1)}), bf16[8,40,7168]{2,1,0:T(8,128)(2,1)}, u32[]{:S(2)}, u32[]{:S(2)}) async-start(bf16[8,40,7168]{2,1,0:T(8,128)(2,1)} %bitcast.113), calls=%async_computation.3 | async-start | bytes 9175040 | tf_op jit(solution)/shard_map/all_to_all | solution.py:65
  265.2 3.5 convolution_multiply_fusion.2
  268.6 4.8 %fusion.6 = bf16[1,128,7168]{2,1,0:T(8,128)(2,1)} fusion(f32[128,7168]{1,0:T(8,128)S(1)} %convolution_multiply_fusion.2, bf16[320,7168]{1,0:T(8,128)(2,1)} %bitcast.13, f32[128]{0:T(128)S(1)} %get-tuple-element.8, s32[128]{0:T(128)S(1)} %get-tuple-element.11), kind=kOutput, calls=%fused_computation.17 | convolution fusion | flops 589996032 | bytes 10093568 | tf_op jit(solution)/shard_map/dot_general | solution.py:121
  273.4 2.9 collective-permute-start.2
  276.4 46.6 %all-to-all-done.3 = bf16[8,40,7168]{2,1,0:T(8,128)(2,1)} async-done(((bf16[8,40,7168]{2,1,0:T(8,128)(2,1)}), bf16[8,40,7168]{2,1,0:T(8,128)(2,1)}, u32[]{:S(2)}, u32[]{:S(2)}) %all-to-all-start.3) | async-done | bytes 4587552 | tf_op jit(solution)/shard_map/all_to_all | solution.py:65
  323.0 3.6 fusion.5
  326.6 36.8 %collective-permute-start.5 = (bf16[1,128,7168]{2,1,0:T(8,128)(2,1)S(1)}, bf16[1,128,7168]{2,1,0:T(8,128)(2,1)S(1)}, u32[]{:S(2)}, u32[]{:S(2)}) collective-permute-start(bf16[1,128,7168]{2,1,0:T(8,128)(2,1)S(1)} %fusion.5), channel_id=1, source_target_pairs={{0,16},{16,32},{32,48},{48,64},{64,80},{80,96},{96,112},{1,17},{17... | collective-permute-start | bytes 5505032 | tf_op jit(solution)/shard_map/ppermute | solution.py:14
  363.4 0.0 collective-permute-done.2
  363.4 79.4 %collective-permute-done.5 = bf16[1,128,7168]{2,1,0:T(8,128)(2,1)S(1)} collective-permute-done((bf16[1,128,7168]{2,1,0:T(8,128)(2,1)S(1)}, bf16[1,128,7168]{2,1,0:T(8,128)(2,1)S(1)}, u32[]{:S(2)}, u32[]{:S(2)}) %collective-permute-start.5) | collective-permute-done | bytes 1835040 | tf_op jit(solution)/shard_map/ppermute | solution.py:14
  442.8 2.8 copy.27
  445.7 1.2 copy.28
  446.9 0.0 copy-done.1
  (26 shorter events, 0.3 us)
Async XLA Ops:
  0.6 2.6 copy-start
  6.8 8.4 %copy-start.4 = (s32[1,128,2]{1,2,0:T(2,128)S(1)}, s32[1,128,2]{1,2,0:T(2,128)}, u32[]{:S(2)}) copy-start(s32[1,128,2]{1,2,0:T(2,128)} %param.16) | copy-start | bytes 3076
  6.8 8.4 %copy-start.5 = (s32[1,2,4]{2,1,0:T(2,128)S(1)}, s32[1,2,4]{2,1,0:T(2,128)}, u32[]{:S(2)}) copy-start(s32[1,2,4]{2,1,0:T(2,128)} %param.14) | copy-start | bytes 100
  6.8 8.6 %copy-start.6 = (s32[1,2,4]{2,1,0:T(2,128)S(1)}, s32[1,2,4]{2,1,0:T(2,128)}, u32[]{:S(2)}) copy-start(s32[1,2,4]{2,1,0:T(2,128)} %param.18) | copy-start | bytes 100
  6.8 9.1 %copy-start.7 = (f32[1,128,2]{1,2,0:T(2,128)S(1)}, f32[1,128,2]{1,2,0:T(2,128)}, u32[]{:S(2)}) copy-start(f32[1,128,2]{1,2,0:T(2,128)} %param.17) | copy-start | bytes 3076
  6.8 9.1 %copy-start.8 = (f32[1,128,2]{1,2,0:T(2,128)S(1)}, f32[1,128,2]{1,2,0:T(2,128)}, u32[]{:S(2)}) copy-start(f32[1,128,2]{1,2,0:T(2,128)} %param.13) | copy-start | bytes 3076
  6.8 66.6 %copy-start.2 = (bf16[1,128,7168]{2,1,0:T(8,128)(2,1)S(1)}, bf16[1,128,7168]{2,1,0:T(8,128)(2,1)}, u32[]{:S(2)}) copy-start(bf16[1,128,7168]{2,1,0:T(8,128)(2,1)} %param.15) | copy-start | bytes 5505028
  6.8 66.4 %all-to-all-start = ((bf16[8,40,7168]{2,1,0:T(8,128)(2,1)}), bf16[8,40,7168]{2,1,0:T(8,128)(2,1)}, u32[]{:S(2)}, u32[]{:S(2)}) async-start(bf16[8,40,7168]{2,1,0:T(8,128)(2,1)} %bitcast.109), calls=%async_computation | async-start | bytes 9175040 | tf_op jit(solution)/shard_map/all_to_all | solution.py:57
  73.2 70.6 %collective-permute-start = (bf16[320,7168]{1,0:T(8,128)(2,1)}, bf16[320,7168]{1,0:T(8,128)(2,1)}, u32[]{:S(2)}, u32[]{:S(2)}) collective-permute-start(bf16[320,7168]{1,0:T(8,128)(2,1)} %bitcast.9), channel_id=1, source_target_pairs={{0,1},{1,0},{2,3},{3,2},{4,5},{5,4},{6,7},{7,6},{8,9},{9,8},{10,11... | collective-permute-start | bytes 13762568 | tf_op jit(solution)/shard_map/ppermute | solution.py:18
  143.8 14.2 %copy-start.3 = (bf16[1,1,640,512]{3,2,1,0:T(8,128)(2,1)S(1)}, bf16[1,1,640,512]{3,2,1,0:T(8,128)(2,1)}, u32[]{:S(2)}) copy-start(bf16[1,1,640,512]{3,2,1,0:T(8,128)(2,1)} %param.19) | copy-start | bytes 1966084
  143.8 14.2 %collective-permute-start.3 = (bf16[320,7168]{1,0:T(8,128)(2,1)}, bf16[320,7168]{1,0:T(8,128)(2,1)}, u32[]{:S(2)}, u32[]{:S(2)}) collective-permute-start(bf16[320,7168]{1,0:T(8,128)(2,1)} %bitcast.26), channel_id=1, source_target_pairs={{0,1},{1,0},{2,3},{3,2},{4,5},{5,4},{6,7},{7,6},{8,9},{9,8},{10,11... | collective-permute-start | bytes 13762568 | tf_op jit(solution)/shard_map/ppermute | solution.py:18
  157.5 17.6 %collective-permute-start.1 = (bf16[320,7168]{1,0:T(8,128)(2,1)}, bf16[320,7168]{1,0:T(8,128)(2,1)}, u32[]{:S(2)}, u32[]{:S(2)}) collective-permute-start(bf16[320,7168]{1,0:T(8,128)(2,1)} %convolution_convert_fusion.2), channel_id=1, source_target_pairs={{0,1},{1,0},{2,3},{3,2},{4,5},{5,4},{6,7},{7,6},{8,9},{9,8},{10,11... | collective-permute-start | bytes 13762568 | tf_op jit(solution)/shard_map/ppermute | solution.py:18
  158.0 7.4 %slice-start = ((s8[7340032]{0:T(1024)(128)(4,1)}), s8[4194304]{0:T(1024)(128)(4,1)S(1)}, s32[]{:S(2)}) async-start(s8[7340032]{0:T(1024)(128)(4,1)} %bitcast.107), calls=%async_computation.4 | async-start | bytes 8388608
  158.1 7.3 %slice-start.1 = ((s8[7340032]{0:T(1024)(128)(4,1)}), s8[3145728]{0:T(1024)(128)(4,1)S(1)}, s32[]{:S(2)}) async-start(s8[7340032]{0:T(1024)(128)(4,1)} %bitcast.107), calls=%async_computation.5 | async-start | bytes 6291456
  165.4 9.8 %slice-start.2 = ((s8[7340032]{0:T(1024)(128)(4,1)}), s8[4194304]{0:T(1024)(128)(4,1)S(1)}, s32[]{:S(2)}) async-start(s8[7340032]{0:T(1024)(128)(4,1)} %bitcast.111), calls=%async_computation.6 | async-start | bytes 8388608
  170.1 5.1 %slice-start.3 = ((s8[7340032]{0:T(1024)(128)(4,1)}), s8[3145728]{0:T(1024)(128)(4,1)S(1)}, s32[]{:S(2)}) async-start(s8[7340032]{0:T(1024)(128)(4,1)} %bitcast.111), calls=%async_computation.7 | async-start | bytes 6291456
  170.1 26.2 %collective-permute-start.4 = (bf16[320,7168]{1,0:T(8,128)(2,1)}, bf16[320,7168]{1,0:T(8,128)(2,1)}, u32[]{:S(2)}, u32[]{:S(2)}) collective-permute-start(bf16[320,7168]{1,0:T(8,128)(2,1)} %convolution_convert_fusion), channel_id=1, source_target_pairs={{0,1},{1,0},{2,3},{3,2},{4,5},{5,4},{6,7},{7,6},{8,9},{9,8},{10,11... | collective-permute-start | bytes 13762568 | tf_op jit(solution)/shard_map/ppermute | solution.py:18
  182.2 68.2 %all-to-all-start.1 = ((bf16[8,40,7168]{2,1,0:T(8,128)(2,1)}), bf16[8,40,7168]{2,1,0:T(8,128)(2,1)}, u32[]{:S(2)}, u32[]{:S(2)}) async-start(bf16[8,40,7168]{2,1,0:T(8,128)(2,1)} %bitcast.114), calls=%async_computation.1 | async-start | bytes 9175040 | tf_op jit(solution)/shard_map/all_to_all | solution.py:65
  250.4 72.6 %all-to-all-start.3 = ((bf16[8,40,7168]{2,1,0:T(8,128)(2,1)}), bf16[8,40,7168]{2,1,0:T(8,128)(2,1)}, u32[]{:S(2)}, u32[]{:S(2)}) async-start(bf16[8,40,7168]{2,1,0:T(8,128)(2,1)} %bitcast.113), calls=%async_computation.3 | async-start | bytes 9175040 | tf_op jit(solution)/shard_map/all_to_all | solution.py:65
  273.4 90.0 %collective-permute-start.2 = (bf16[1,128,7168]{2,1,0:T(8,128)(2,1)}, bf16[1,128,7168]{2,1,0:T(8,128)(2,1)}, u32[]{:S(2)}, u32[]{:S(2)}) collective-permute-start(bf16[1,128,7168]{2,1,0:T(8,128)(2,1)} %fusion.6), channel_id=1, source_target_pairs={{0,16},{16,32},{32,48},{48,64},{64,80},{80,96},{96,112},{1,17},{17... | collective-permute-start | bytes 5505032 | tf_op jit(solution)/shard_map/ppermute | solution.py:14
  323.0 123.9 %copy-start.1 = (bf16[1,128,7168]{2,1,0:T(8,128)(2,1)S(1)}, bf16[1,128,7168]{2,1,0:T(8,128)(2,1)}, u32[]{:S(2)}) copy-start(bf16[1,128,7168]{2,1,0:T(8,128)(2,1)} %param.11) | copy-start | bytes 5505028
  326.6 116.2 %collective-permute-start.5 = (bf16[1,128,7168]{2,1,0:T(8,128)(2,1)S(1)}, bf16[1,128,7168]{2,1,0:T(8,128)(2,1)S(1)}, u32[]{:S(2)}, u32[]{:S(2)}) collective-permute-start(bf16[1,128,7168]{2,1,0:T(8,128)(2,1)S(1)} %fusion.5), channel_id=1, source_target_pairs={{0,16},{16,32},{32,48},{48,64},{64,80},{80,96},{96,112},{1,17},{17... | collective-permute-start | bytes 5505032 | tf_op jit(solution)/shard_map/ppermute | solution.py:14

commit v2 on v1

v2 whole, which is shorter than its diff:
```python
import functools

import jax
import jax.experimental.pallas as pl
import jax.experimental.pallas.tpu as pltpu
import jax.numpy as jnp
from jax import lax
from jax.sharding import PartitionSpec as P

keep_scale = 1.0 / 0.9
root_half = 0.7071067811865476
inv_root_tau = 0.3989422804014327
MESH = pl.DeviceIdType.MESH
CHUNK = 1024


def gelu_value(h):
    return h * (0.5 * (1.0 + lax.erf(h * root_half)))


def gelu_slope(h):
    return 0.5 * (1.0 + lax.erf(h * root_half)) + h * inv_root_tau * jnp.exp(-0.5 * h * h)


def unpack_keep(words):
    shifts = jnp.arange(32, dtype=jnp.int32)
    bits = jnp.right_shift(words[:, :, None], shifts[None, None, :]) & 1
    return bits.reshape(words.shape[0], words.shape[1] * 32).T.astype(jnp.float32)


def routing(ids, owners, cap):
    names = jnp.arange(owners, dtype=jnp.int32)
    named = ids[:, :, None] == names[None, None, :]
    hit = jnp.any(named, axis=1).astype(jnp.int32)
    place = jnp.cumsum(hit, axis=0) - 1
    seat = jnp.sum(jnp.where(named, place[:, None, :], 0), axis=2)
    return ids * cap + seat


def relay(
    sizes,
    send_one, send_two, meta, saved, w_in, w_out,
    out_one, out_two, back_one, back_two,
    wi, wo, got_one, got_two, other_one, other_two, acc, act, pre, metas, zeros, staged, held,
    load_sem, meta_sem, d_send, d_recv, s_send, s_recv, x_send, x_recv, c_send, c_recv,
    r_sem, o_send, o_recv,
):
    owners, cap, steps, width, sections = sizes
    rows = owners * cap
    p, me, core = lax.axis_index("pipe"), lax.axis_index("expert"), lax.axis_index("dp")
    odd = lax.rem(p, 2)
    across = p + 1 - 2 * odd
    sends_on = jnp.logical_and(odd == 0, p + 2 < sections)
    gets_on = jnp.logical_and(odd == 0, p >= 2)

    barrier = pltpu.get_barrier_semaphore()
    for d in range(1, owners):
        pl.semaphore_signal(
            barrier, device_id=(p, lax.rem(me + d, owners), core), device_id_type=MESH
        )
    for d in range(owners):
        pl.semaphore_signal(
            barrier, device_id=(across, lax.rem(me + d, owners), core), device_id_type=MESH
        )
    pl.semaphore_signal(barrier, device_id=(p, me, 1 - core), device_id_type=MESH)

    @pl.when(gets_on)
    def _():
        pl.semaphore_signal(barrier, device_id=(p - 2, me, core), device_id_type=MESH)

    load_in = pltpu.make_async_copy(w_in, wi, load_sem.at[0])
    load_out = pltpu.make_async_copy(w_out, wo, load_sem.at[1])
    load_pre = [
        pltpu.make_async_copy(saved.at[:, core if side == 0 else 1 - core], pre.at[side], load_sem.at[2 + side])
        for side in range(2)
    ]
    load_in.start()
    load_out.start()
    for copy in load_pre:
        copy.start()
    zeros[...] = jnp.zeros_like(zeros)

    pl.semaphore_wait(barrier, 2 * owners + jnp.where(sends_on, 1, 0))

    sends, gots, others = (send_one, send_two), (got_one, got_two), (other_one, other_two)
    backs, outs = (back_one, back_two), (out_one, out_two)

    def columns(j):
        return pl.ds(pl.multiple_of(j * width, width), width)

    def dispatch(m, j):
        for d in range(1, owners):
            to = lax.rem(me + d, owners)
            pltpu.make_async_remote_copy(
                sends[m].at[to, :, columns(j)], gots[m].at[j, 0, me],
                d_send.at[m, j], d_recv.at[m, j],
                device_id=(p, to, core), device_id_type=MESH,
            ).start()
        pltpu.make_async_copy(
            sends[m].at[me, :, columns(j)], gots[m].at[j, 0, me], d_recv.at[m, j]
        ).start()

    def swap(m, j):
        return pltpu.make_async_remote_copy(
            gots[m].at[j, 0], gots[m].at[j, 1], s_send.at[m, j], s_recv.at[m, j],
            device_id=(p, me, 1 - core), device_id_type=MESH,
        )

    def cross(m, j):
        return pltpu.make_async_remote_copy(
            gots[m].at[j, 1], others[m].at[j], x_send.at[m, j], x_recv.at[m, j],
            device_id=(p, me, 1 - core), device_id_type=MESH,
        )

    def whole(ref, sem):
        return pltpu.make_async_copy(ref, ref, sem)

    def flat(ref):
        return ref[...].reshape(rows, width)

    def receive(m, j):
        whole(gots[m].at[j, 0], d_recv.at[m, j]).wait()
        swap(m, j).start()
        for side in range(2):
            if side == 1:
                swap(m, j).wait()
            block = flat(gots[m].at[j, side])
            if m == 0:
                acc[m, side] += jnp.dot(
                    block, wi[columns(j), :], preferred_element_type=jnp.float32
                )
            else:
                acc[m, side] += lax.dot_general(
                    block, wo[:, columns(j)], (((1,), (1,)), ((), ())),
                    preferred_element_type=jnp.float32,
                )

    def project(m, j, side):
        if m == 0:
            part = jnp.dot(act[m, side], wo[:, columns(j)], preferred_element_type=jnp.float32)
        else:
            part = lax.dot_general(
                act[m, side], wi[columns(j), :], (((1,), (1,)), ((), ())),
                preferred_element_type=jnp.float32,
            )
        return part.reshape(owners, cap, width).astype(jnp.bfloat16)

    def give_back(m, j):
        gots[m][j, 1] = project(m, j, 1)
        cross(m, j).start()
        part = project(m, j, 0)
        cross(m, j).wait()
        gots[m][j, 0] = (
            part.astype(jnp.float32) + others[m][j].astype(jnp.float32)
        ).astype(jnp.bfloat16)
        for d in range(owners):
            to = lax.rem(me + d, owners)
            pltpu.make_async_remote_copy(
                gots[m].at[j, 0, to], backs[m].at[j, me], c_send.at[m, j], c_recv.at[m, j],
                device_id=(across, to, core), device_id_type=MESH,
            ).start()

    def out_local(m, j):
        return pltpu.make_async_copy(staged.at[m, j], outs[m].at[:, columns(j)], o_send.at[m, j])

    def out_zero(m, j):
        return pltpu.make_async_copy(zeros, outs[m].at[:, columns(j)], o_recv.at[m, j])

    def out_on(m, j):
        return pltpu.make_async_remote_copy(
            staged.at[m, j], outs[m].at[:, columns(j)], o_send.at[m, j], o_recv.at[m, j],
            device_id=(lax.rem(p + 2, sections), me, core), device_id_type=MESH,
        )

    def collect(m, j):
        whole(backs[m].at[j], c_recv.at[m, j]).wait()
        fetch = pltpu.make_async_copy(backs[m].at[j], held, r_sem)
        fetch.start()
        seats = lax.broadcasted_iota(jnp.int32, (metas.shape[1], rows), 1).astype(jnp.float32)
        base = 4 * m
        hot = [(metas[1, :, base + k : base + k + 1] == seats) for k in range(2)]
        fetch.wait()
        block = flat(held)

        def rows_of(mask):
            return jnp.dot(
                jnp.where(mask, 1.0, 0.0).astype(jnp.bfloat16), block,
                preferred_element_type=jnp.float32,
            )

        if m == 0:
            total = (
                metas[1, :, base + 2 : base + 3] * rows_of(hot[0])
                + metas[1, :, base + 3 : base + 4] * rows_of(hot[1])
            )
        else:
            total = rows_of(jnp.logical_or(hot[0], hot[1]))
        staged[m, j] = total.astype(jnp.bfloat16)

        @pl.when(odd == 1)
        def _():
            out_local(m, j).start()

        @pl.when(sends_on)
        def _():
            out_on(m, j).start()

        @pl.when(p == 0)
        def _():
            out_zero(m, j).start()

    def loop(body):
        lax.fori_loop(0, steps, lambda j, _: (body(j), 0)[1], 0)

    meta_local = pltpu.make_async_copy(meta, metas.at[0], meta_sem.at[2])
    meta_far = pltpu.make_async_remote_copy(
        meta, metas.at[1], meta_sem.at[0], meta_sem.at[1],
        device_id=(across, me, core), device_id_type=MESH,
    )
    meta_local.start()
    loop(lambda j: dispatch(0, j))
    meta_far.start()
    acc[...] = jnp.zeros_like(acc)
    load_in.wait()

    def first(j):
        dispatch(1, j)
        receive(0, j)

    loop(first)
    for side in range(2):
        act[0, side] = gelu_value(acc[0, side]).astype(jnp.bfloat16)
    load_out.wait()

    def second(j):
        give_back(0, j)
        receive(1, j)

    loop(second)
    for copy in load_pre:
        copy.wait()
    for side in range(2):
        slope = gelu_slope(pre[side].astype(jnp.float32)).reshape(rows, pre.shape[3])
        act[1, side] = (acc[1, side] * slope).astype(jnp.bfloat16)
    meta_local.wait()
    meta_far.wait()

    def third(j):
        give_back(1, j)
        collect(0, j)

    loop(third)
    loop(lambda j: collect(1, j))

    def drain(j):
        for m in range(2):
            part = gots[m].at[j, 0]
            whole(part.at[pl.ds(0, owners - 1)], d_send.at[m, j]).wait()
            whole(part, c_send.at[m, j]).wait()

            @pl.when(odd == 1)
            def _():
                out_local(m, j).wait()

            @pl.when(sends_on)
            def _():
                out_on(m, j).wait_send()

            @pl.when(gets_on)
            def _():
                out_on(m, j).wait_recv()

            @pl.when(p == 0)
            def _():
                out_zero(m, j).wait()

    loop(drain)


def local(
    rising_in,
    rising_ids,
    rising_gates,
    rising_drop,
    sinking_grad,
    sinking_ids,
    sinking_gates,
    sinking_drop,
    sinking_pre,
    w_in,
    w_out,
):
    owners, pairs, sections = lax.axis_size("expert"), lax.axis_size("dp"), lax.axis_size("pipe")
    slots, half = sinking_pre.shape[2:]
    count, model = rising_in.shape[1:]
    cap = slots // (owners * pairs)
    rows = owners * cap
    width = CHUNK
    steps = model // width
    coef_one = unpack_keep(rising_drop[0]) * rising_gates[0] * keep_scale
    coef_two = unpack_keep(sinking_drop[0]) * sinking_gates[0] * keep_scale
    seats_one = routing(rising_ids[0], owners, cap)
    seats_two = routing(sinking_ids[0], owners, cap)
    meta = jnp.concatenate(
        [
            seats_one.astype(jnp.float32), coef_one, seats_two.astype(jnp.float32), coef_two,
            jnp.zeros((count, 120), jnp.float32),
        ],
        axis=1,
    )

    def hot(seats, k):
        return seats[:, k : k + 1] == jnp.arange(rows, dtype=jnp.int32)[None, :]

    def spread(mask, values):
        return lax.dot_general(
            mask.astype(jnp.bfloat16), values, (((0,), (0,)), ((), ())),
            preferred_element_type=jnp.float32,
        )

    send_one = spread(hot(seats_one, 0) | hot(seats_one, 1), rising_in[0]).astype(jnp.bfloat16)
    weight = jnp.sum(
        sum(jnp.where(hot(seats_two, k), coef_two[:, k : k + 1], 0.0) for k in range(2)), axis=0
    )
    send_two = (
        weight[:, None] * spread(hot(seats_two, 0) | hot(seats_two, 1), sinking_grad[0])
    ).astype(jnp.bfloat16)

    hbm = pl.BlockSpec(memory_space=pl.ANY)
    b16, f32 = jnp.bfloat16, jnp.float32
    dma = pltpu.SemaphoreType.DMA
    result = pl.pallas_call(
        functools.partial(relay, (owners, cap, steps, width, sections)),
        out_shape=(
            jax.ShapeDtypeStruct((count, model), b16),
            jax.ShapeDtypeStruct((count, model), b16),
            jax.ShapeDtypeStruct((steps, owners, cap, width), b16),
            jax.ShapeDtypeStruct((steps, owners, cap, width), b16),
        ),
        in_specs=[hbm] * 6,
        out_specs=(hbm,) * 4,
        scratch_shapes=[
            pltpu.VMEM((model, half), b16),
            pltpu.VMEM((half, model), b16),
            pltpu.VMEM((steps, 2, owners, cap, width), b16),
            pltpu.VMEM((steps, 2, owners, cap, width), b16),
            pltpu.VMEM((steps, owners, cap, width), b16),
            pltpu.VMEM((steps, owners, cap, width), b16),
            pltpu.VMEM((2, 2, rows, half), f32),
            pltpu.VMEM((2, 2, rows, half), b16),
            pltpu.VMEM((2, owners, cap, half), b16),
            pltpu.VMEM((2, count, 128), f32),
            pltpu.VMEM((count, width), b16),
            pltpu.VMEM((2, steps, count, width), b16),
            pltpu.VMEM((owners, cap, width), b16),
            dma((4,)),
            dma((3,)),
        ]
        + [dma((2, steps))] * 8
        + [dma, dma((2, steps)), dma((2, steps))],
        compiler_params=pltpu.CompilerParams(
            collective_id=0, has_side_effects=True, vmem_limit_bytes=62 << 20
        ),
        cost_estimate=pl.CostEstimate(
            flops=16 * rows * model * half, bytes_accessed=60_000_000, transcendentals=4 * rows * half
        ),
    )(
        send_one.reshape(owners, cap, model),
        send_two.reshape(owners, cap, model),
        meta,
        sinking_pre.reshape(owners, pairs, cap, half),
        w_in[0, 0],
        w_out[0, 0],
    )
    return (result[0][None], result[1][None])


def solution(mesh):
    placed = (
        P("pipe", ("expert", "dp"), None),
        P("pipe", ("expert", "dp"), None),
        P("pipe", ("expert", "dp"), None),
        P("pipe", None, ("expert", "dp")),
        P("pipe", ("expert", "dp"), None),
        P("pipe", ("expert", "dp"), None),
        P("pipe", ("expert", "dp"), None),
        P("pipe", None, ("expert", "dp")),
        P("pipe", "expert", None, "dp"),
        P("pipe", "expert", None, "dp"),
        P("pipe", "expert", "dp", None),
    )
    return jax.shard_map(
        local,
        mesh=mesh,
        in_specs=placed,
        out_specs=(P("pipe", ("expert", "dp"), None), P("pipe", ("expert", "dp"), None)),
        check_vma=False,
    )
```

time: 448 us -> 245 us (0.55)
  the two profiles are of different devices: /device:TPU:20 before, /device:TPU:24 now
where the time goes in v2:
time: 245 us; the launch traced here: 244 us
  Pallas kernels  225 us (92%)
  local copies, waits for them, and re-layouts  11.1 us (5%)
  matrix products  7.01 us (3%)
    pallas_call x1, Pallas kernels, local(): pl.pallas_call(functools.partial(relay, (owners, cap, steps, width, secti...  225 us
    unnamed x12, local copies, waits for them, and re-layouts  7.38 us
    dot_general x2, matrix products, spread(): lax.dot_general(mask.astype(jnp.bfloat16), values, (((0,), (0,)), ((), ()...  7.01 us

profile of v2, /device:TPU:24, one launch (start us, length us, event | category | flops | bytes accessed | tf_op | source)
XLA Modules:
  0.0 244.1 jit_solution(14593267161049488748)
XLA Ops:
  0.6 0.0 copy-start
  0.6 0.9 copy.37
  1.5 0.8 copy.35
  2.3 0.1 shift_right_arithmetic.48
  2.4 0.8 copy.25
  3.2 0.1 copy.26
  3.3 0.1 copy.27
  3.4 0.2 reduce_window_sum.17
  3.6 0.1 copy.29
  3.8 0.8 copy.30
  4.6 0.1 copy.31
  4.6 0.1 copy.32
  4.8 0.2 reduce_window_sum.18
  5.0 0.1 copy.34
  5.2 0.2 slice_reduce_fusion.3
  5.4 0.2 slice_reduce_fusion.5
  5.5 0.8 copy.38
  6.3 0.8 copy.36
  7.1 0.1 fusion.11
  7.2 0.2 slice_reduce_fusion.2
  7.4 0.2 add_reduce_fusion
  7.6 0.8 concatenate.3.meta
  8.3 0.0 copy-done
  8.3 0.0 copy-start.2
  8.3 3.5 %fusion = bf16[320,7168]{1,0:T(8,128)(2,1)} fusion(f32[320]{0:T(512)S(1)} %add_reduce_fusion, bf16[1,128,7168]{2,1,0:T(8,128)(2,1)S(1)} %copy-done, s32[128]{0:T(128)S(1)} %get-tuple-element.7, s32[128]{0:T(128)S(1)} %get-tuple-element.6), kind=kOutput, calls=%fused_computation.1 | convolution fusion | flops 591912960 | bytes 6424832 | tf_op jit(solution)/shard_map/dot_general | solution.py:316
  11.8 0.0 copy-done.2
  11.8 3.5 %convolution_convert_fusion = bf16[320,7168]{1,0:T(8,128)(2,1)} fusion(bf16[1,128,7168]{2,1,0:T(8,128)(2,1)S(1)} %copy-done.2, s32[128]{0:T(128)S(1)} %get-tuple-element.11, s32[128]{0:T(128)S(1)} %get-tuple-element.10), kind=kOutput, calls=%fused_computation.2 | convolution fusion | flops 589619200 | bytes 6423552 | tf_op jit(solution)/shard_map/dot_general | solution.py:316
  15.3 224.5 %shard_map.122 = (bf16[128,7168]{1,0:T(8,128)(2,1)}, bf16[128,7168]{1,0:T(8,128)(2,1)}, bf16[7,8,40,1024]{3,2,1,0:T(8,128)(2,1)}, bf16[7,8,40,1024]{3,2,1,0:T(8,128)(2,1)}) custom-call(bf16[8,40,7168]{2,1,0:T(8,128)(2,1)} %bitcast.50, bf16[8,40,7168]{2,1,0:T(8,128)(2,1)} %bitcast.49, f32[128,128]{1,0:T(8,128)} %concatenate.3.meta, ...), custom_call_target="tpu_custom_call" | custom-call | flops 18790481920 | bytes 60000000 | tf_op jit(solution)/shard_map/pallas_call | solution.py:332
  239.9 0.0 copy-start.1
  239.9 3.0 %copy.41 = bf16[1,128,7168]{2,1,0:T(8,128)(2,1)} copy(bf16[1,128,7168]{2,1,0:T(8,128)(2,1)} %bitcast.52) | data formatting | bytes 3670016
  242.9 0.0 copy-done.1
  242.9 1.2 copy.42
  (13 shorter events, 0.2 us)
Async XLA Ops:
  0.6 7.7 %copy-start = (bf16[1,128,7168]{2,1,0:T(8,128)(2,1)S(1)}, bf16[1,128,7168]{2,1,0:T(8,128)(2,1)}, u32[]{:S(2)}) copy-start(bf16[1,128,7168]{2,1,0:T(8,128)(2,1)} %param.15) | copy-start | bytes 5505028
  8.3 3.5 %copy-start.2 = (bf16[1,128,7168]{2,1,0:T(8,128)(2,1)S(1)}, bf16[1,128,7168]{2,1,0:T(8,128)(2,1)}, u32[]{:S(2)}) copy-start(bf16[1,128,7168]{2,1,0:T(8,128)(2,1)} %param.11) | copy-start | bytes 5505028
  239.9 3.0 %copy-start.1 = (bf16[128,7168]{1,0:T(8,128)(2,1)S(1)}, bf16[128,7168]{1,0:T(8,128)(2,1)}, u32[]{:S(2)}) copy-start(bf16[128,7168]{1,0:T(8,128)(2,1)} %get-tuple-element.5) | copy-start | bytes 5505028

commit v3 on v2

--- a/solution.py
+++ b/solution.py
@@ -11,7 +11,7 @@
 root_half = 0.7071067811865476
 inv_root_tau = 0.3989422804014327
 MESH = pl.DeviceIdType.MESH
-CHUNK = 1024
+CHUNK = 512
 
 
 def gelu_value(h):
@@ -22,28 +22,43 @@
     return 0.5 * (1.0 + lax.erf(h * root_half)) + h * inv_root_tau * jnp.exp(-0.5 * h * h)
 
 
-def unpack_keep(words):
-    shifts = jnp.arange(32, dtype=jnp.int32)
-    bits = jnp.right_shift(words[:, :, None], shifts[None, None, :]) & 1
-    return bits.reshape(words.shape[0], words.shape[1] * 32).T.astype(jnp.float32)
+def coefficients(words, gates):
+    lanes = lax.broadcasted_iota(jnp.int32, gates.shape, 1)
+    word = jnp.zeros(gates.shape, jnp.int32)
+    for q in range(words.shape[1]):
+        word = jnp.where(lanes // 32 == q, words[:, q : q + 1], word)
+    keep = (jnp.right_shift(word, lanes % 32) & 1).astype(jnp.float32)
+    return keep * gates * keep_scale
 
 
 def routing(ids, owners, cap):
-    names = jnp.arange(owners, dtype=jnp.int32)
-    named = ids[:, :, None] == names[None, None, :]
-    hit = jnp.any(named, axis=1).astype(jnp.int32)
-    place = jnp.cumsum(hit, axis=0) - 1
-    seat = jnp.sum(jnp.where(named, place[:, None, :], 0), axis=2)
-    return ids * cap + seat
+    top, count = ids.shape
+    names = lax.broadcasted_iota(jnp.int32, (owners, count), 0)
+    named = [ids[k : k + 1, :] == names for k in range(top)]
+    hit = jnp.where(jnp.logical_or(named[0], named[1]), 1.0, 0.0)
+    upto = lax.broadcasted_iota(jnp.int32, (count, count), 0) <= lax.broadcasted_iota(
+        jnp.int32, (count, count), 1
+    )
+    place = jnp.dot(hit, jnp.where(upto, 1.0, 0.0), preferred_element_type=jnp.float32)
+    row = place - 1.0 + (names * cap).astype(jnp.float32)
+    return [jnp.sum(jnp.where(n, row, 0.0), axis=0, keepdims=True) for n in named]
+
+
+def upright(row):
+    n = row.shape[1]
+    same = lax.broadcasted_iota(jnp.int32, (n, n), 0) == lax.broadcasted_iota(jnp.int32, (n, n), 1)
+    return jnp.sum(jnp.where(same, row, 0.0), axis=1, keepdims=True)
 
 
 def relay(
     sizes,
-    send_one, send_two, meta, saved, w_in, w_out,
-    out_one, out_two, back_one, back_two,
-    wi, wo, got_one, got_two, other_one, other_two, acc, act, pre, metas, zeros, staged, held,
+    ids_one, gates_one, drop_one, ids_two, gates_two, drop_two,
+    rows_one, rows_two, saved, w_in, w_out,
+    out_one, out_two,
+    wi, wo, got_one, got_two, other_one, other_two, back_one, back_two,
+    acc, act, pre, metas, zeros, staged, put, scale, hot, coef,
     load_sem, meta_sem, d_send, d_recv, s_send, s_recv, x_send, x_recv, c_send, c_recv,
-    r_sem, o_send, o_recv,
+    o_send, o_recv, l_sem,
 ):
     owners, cap, steps, width, sections = sizes
     rows = owners * cap
@@ -74,30 +89,63 @@
         pltpu.make_async_copy(saved.at[:, core if side == 0 else 1 - core], pre.at[side], load_sem.at[2 + side])
         for side in range(2)
     ]
+    tokens = (rows_one, rows_two)
+
+    def columns(j):
+        return pl.ds(pl.multiple_of(j * width, width), width)
+
+    def load_rows(m, j):
+        return pltpu.make_async_copy(tokens[m].at[:, columns(j)], staged.at[m, j], l_sem.at[m, j])
+
+    def loop(body):
+        lax.fori_loop(0, steps, lambda j, _: (body(j), 0)[1], 0)
+
+    loop(lambda j: load_rows(0, j).start())
     load_in.start()
+    loop(lambda j: load_rows(1, j).start())
     load_out.start()
     for copy in load_pre:
         copy.start()
+
+    count = metas.shape[2]
+    places = lax.broadcasted_iota(jnp.int32, (rows, count), 0).astype(jnp.float32)
+    for m, (ids, gates, words) in enumerate(
+        ((ids_one, gates_one, drop_one), (ids_two, gates_two, drop_two))
+    ):
+        seats = routing(ids[...], owners, cap)
+        weights = coefficients(words[...], gates[...])
+        mine = [places == seat for seat in seats]
+        put[m] = jnp.where(jnp.logical_or(mine[0], mine[1]), 1.0, 0.0).astype(jnp.bfloat16)
+        for k in range(2):
+            metas[0, 4 * m + k : 4 * m + k + 1, :] = seats[k]
+        metas[0, 4 * m + 2 : 4 * m + 4, :] = weights
+        if m == 1:
+            scale[...] = jnp.sum(
+                jnp.where(mine[0], weights[0:1], 0.0) + jnp.where(mine[1], weights[1:2], 0.0),
+                axis=1, keepdims=True,
+            )
     zeros[...] = jnp.zeros_like(zeros)
 
     pl.semaphore_wait(barrier, 2 * owners + jnp.where(sends_on, 1, 0))
 
-    sends, gots, others = (send_one, send_two), (got_one, got_two), (other_one, other_two)
+    gots, others = (got_one, got_two), (other_one, other_two)
     backs, outs = (back_one, back_two), (out_one, out_two)
 
-    def columns(j):
-        return pl.ds(pl.multiple_of(j * width, width), width)
-
     def dispatch(m, j):
+        load_rows(m, j).wait()
+        picked = jnp.dot(put[m], staged[m, j], preferred_element_type=jnp.float32)
+        if m == 1:
+            picked = scale[...] * picked
+        others[m][j] = picked.reshape(owners, cap, width).astype(jnp.bfloat16)
         for d in range(1, owners):
             to = lax.rem(me + d, owners)
             pltpu.make_async_remote_copy(
-                sends[m].at[to, :, columns(j)], gots[m].at[j, 0, me],
+                others[m].at[j, to], gots[m].at[j, 0, me],
                 d_send.at[m, j], d_recv.at[m, j],
                 device_id=(p, to, core), device_id_type=MESH,
             ).start()
         pltpu.make_async_copy(
-            sends[m].at[me, :, columns(j)], gots[m].at[j, 0, me], d_recv.at[m, j]
+            others[m].at[j, me], gots[m].at[j, 0, me], d_recv.at[m, j]
         ).start()
 
     def swap(m, j):
@@ -119,6 +167,7 @@
         return ref[...].reshape(rows, width)
 
     def receive(m, j):
+        whole(others[m].at[j, pl.ds(0, owners - 1)], d_send.at[m, j]).wait()
         whole(gots[m].at[j, 0], d_recv.at[m, j]).wait()
         swap(m, j).start()
         for side in range(2):
@@ -174,27 +223,15 @@
 
     def collect(m, j):
         whole(backs[m].at[j], c_recv.at[m, j]).wait()
-        fetch = pltpu.make_async_copy(backs[m].at[j], held, r_sem)
-        fetch.start()
-        seats = lax.broadcasted_iota(jnp.int32, (metas.shape[1], rows), 1).astype(jnp.float32)
-        base = 4 * m
-        hot = [(metas[1, :, base + k : base + k + 1] == seats) for k in range(2)]
-        fetch.wait()
-        block = flat(held)
-
-        def rows_of(mask):
-            return jnp.dot(
-                jnp.where(mask, 1.0, 0.0).astype(jnp.bfloat16), block,
-                preferred_element_type=jnp.float32,
-            )
+        block = flat(backs[m].at[j])
+
+        def rows_of(n):
+            return jnp.dot(hot[n], block, preferred_element_type=jnp.float32)
 
         if m == 0:
-            total = (
-                metas[1, :, base + 2 : base + 3] * rows_of(hot[0])
-                + metas[1, :, base + 3 : base + 4] * rows_of(hot[1])
-            )
+            total = coef[0] * rows_of(0) + coef[1] * rows_of(1)
         else:
-            total = rows_of(jnp.logical_or(hot[0], hot[1]))
+            total = rows_of(2)
         staged[m, j] = total.astype(jnp.bfloat16)
 
         @pl.when(odd == 1)
@@ -209,15 +246,10 @@
         def _():
             out_zero(m, j).start()
 
-    def loop(body):
-        lax.fori_loop(0, steps, lambda j, _: (body(j), 0)[1], 0)
-
-    meta_local = pltpu.make_async_copy(meta, metas.at[0], meta_sem.at[2])
     meta_far = pltpu.make_async_remote_copy(
-        meta, metas.at[1], meta_sem.at[0], meta_sem.at[1],
+        metas.at[0], metas.at[1], meta_sem.at[0], meta_sem.at[1],
         device_id=(across, me, core), device_id_type=MESH,
     )
-    meta_local.start()
     loop(lambda j: dispatch(0, j))
     meta_far.start()
     acc[...] = jnp.zeros_like(acc)
@@ -242,8 +274,16 @@
     for side in range(2):
         slope = gelu_slope(pre[side].astype(jnp.float32)).reshape(rows, pre.shape[3])
         act[1, side] = (acc[1, side] * slope).astype(jnp.bfloat16)
-    meta_local.wait()
     meta_far.wait()
+    seat_at = lax.broadcasted_iota(jnp.int32, (count, rows), 1).astype(jnp.float32)
+
+    def theirs(n):
+        return seat_at == upright(metas[1, n : n + 1, :])
+
+    for k in range(2):
+        hot[k] = jnp.where(theirs(k), 1.0, 0.0).astype(jnp.bfloat16)
+        coef[k] = upright(metas[1, 2 + k : 3 + k, :])
+    hot[2] = jnp.where(jnp.logical_or(theirs(4), theirs(5)), 1.0, 0.0).astype(jnp.bfloat16)
 
     def third(j):
         give_back(1, j)
@@ -255,7 +295,6 @@
     def drain(j):
         for m in range(2):
             part = gots[m].at[j, 0]
-            whole(part.at[pl.ds(0, owners - 1)], d_send.at[m, j]).wait()
             whole(part, c_send.at[m, j]).wait()
 
             @pl.when(odd == 1)
@@ -297,35 +336,6 @@
     rows = owners * cap
     width = CHUNK
     steps = model // width
-    coef_one = unpack_keep(rising_drop[0]) * rising_gates[0] * keep_scale
-    coef_two = unpack_keep(sinking_drop[0]) * sinking_gates[0] * keep_scale
-    seats_one = routing(rising_ids[0], owners, cap)
-    seats_two = routing(sinking_ids[0], owners, cap)
-    meta = jnp.concatenate(
-        [
-            seats_one.astype(jnp.float32), coef_one, seats_two.astype(jnp.float32), coef_two,
-            jnp.zeros((count, 120), jnp.float32),
-        ],
-        axis=1,
-    )
-
-    def hot(seats, k):
-        return seats[:, k : k + 1] == jnp.arange(rows, dtype=jnp.int32)[None, :]
-
-    def spread(mask, values):
-        return lax.dot_general(
-            mask.astype(jnp.bfloat16), values, (((0,), (0,)), ((), ())),
-            preferred_element_type=jnp.float32,
-        )
-
-    send_one = spread(hot(seats_one, 0) | hot(seats_one, 1), rising_in[0]).astype(jnp.bfloat16)
-    weight = jnp.sum(
-        sum(jnp.where(hot(seats_two, k), coef_two[:, k : k + 1], 0.0) for k in range(2)), axis=0
-    )
-    send_two = (
-        weight[:, None] * spread(hot(seats_two, 0) | hot(seats_two, 1), sinking_grad[0])
-    ).astype(jnp.bfloat16)
-
     hbm = pl.BlockSpec(memory_space=pl.ANY)
     b16, f32 = jnp.bfloat16, jnp.float32
     dma = pltpu.SemaphoreType.DMA
@@ -334,11 +344,9 @@
         out_shape=(
             jax.ShapeDtypeStruct((count, model), b16),
             jax.ShapeDtypeStruct((count, model), b16),
-            jax.ShapeDtypeStruct((steps, owners, cap, width), b16),
-            jax.ShapeDtypeStruct((steps, owners, cap, width), b16),
         ),
-        in_specs=[hbm] * 6,
-        out_specs=(hbm,) * 4,
+        in_specs=[pl.BlockSpec(memory_space=pltpu.VMEM)] * 6 + [hbm] * 5,
+        out_specs=(hbm,) * 2,
         scratch_shapes=[
             pltpu.VMEM((model, half), b16),
             pltpu.VMEM((half, model), b16),
@@ -346,18 +354,22 @@
             pltpu.VMEM((steps, 2, owners, cap, width), b16),
             pltpu.VMEM((steps, owners, cap, width), b16),
             pltpu.VMEM((steps, owners, cap, width), b16),
+            pltpu.VMEM((steps, owners, cap, width), b16),
+            pltpu.VMEM((steps, owners, cap, width), b16),
             pltpu.VMEM((2, 2, rows, half), f32),
             pltpu.VMEM((2, 2, rows, half), b16),
             pltpu.VMEM((2, owners, cap, half), b16),
-            pltpu.VMEM((2, count, 128), f32),
+            pltpu.VMEM((2, 8, count), f32),
             pltpu.VMEM((count, width), b16),
             pltpu.VMEM((2, steps, count, width), b16),
-            pltpu.VMEM((owners, cap, width), b16),
+            pltpu.VMEM((2, rows, count), b16),
+            pltpu.VMEM((rows, 1), f32),
+            pltpu.VMEM((3, count, rows), b16),
+            pltpu.VMEM((2, count, 1), f32),
             dma((4,)),
-            dma((3,)),
+            dma((2,)),
         ]
-        + [dma((2, steps))] * 8
-        + [dma, dma((2, steps)), dma((2, steps))],
+        + [dma((2, steps))] * 11,
         compiler_params=pltpu.CompilerParams(
             collective_id=0, has_side_effects=True, vmem_limit_bytes=62 << 20
         ),
@@ -365,9 +377,14 @@
             flops=16 * rows * model * half, bytes_accessed=60_000_000, transcendentals=4 * rows * half
         ),
     )(
-        send_one.reshape(owners, cap, model),
-        send_two.reshape(owners, cap, model),
-        meta,
+        rising_ids[0].T,
+        rising_gates[0].T,
+        rising_drop[0],
+        sinking_ids[0].T,
+        sinking_gates[0].T,
+        sinking_drop[0],
+        rising_in[0],
+        sinking_grad[0],
         sinking_pre.reshape(owners, pairs, cap, half),
         w_in[0, 0],
         w_out[0, 0],

time: 245 us -> 221 us (0.902)
  Pallas kernels: 225 us -> 216 us
  matrix products: 7.01 us -> 0 us
  local copies, waits for them, and re-layouts: 11.1 us -> 4.21 us
    pallas_call x1, Pallas kernels: 225 us -> 216 us  [local(): pl.pallas_call(functools.partial(relay, (owners, cap, steps, width, secti...]
    dot_general x2 -> x0, matrix products: 7.01 us -> none  [spread(): lax.dot_general(mask.astype(jnp.bfloat16), values, (((0,), (0,)), ((), ()...]
    unnamed x12 -> x4, local copies, waits for them, and re-layouts: 7.38 us -> 4.21 us
where the time goes in v3:
time: 221 us
  Pallas kernels  216 us (98%)
  local copies, waits for them, and re-layouts  4.21 us (2%)
    pallas_call x1, Pallas kernels, local(): pl.pallas_call(functools.partial(relay, (owners, cap, steps, width, secti...  216 us

profile of v3, /device:TPU:24, one launch (start us, length us, event | category | flops | bytes accessed | tf_op | source)
XLA Modules:
  0.0 221.2 jit_solution(13435663686027133028)
XLA Ops:
  0.6 216.3 %shard_map.122 = (bf16[128,7168]{1,0:T(8,128)(2,1)}, bf16[128,7168]{1,0:T(8,128)(2,1)}) custom-call(s32[2,128]{1,0:T(2,128)} %bitcast.28, f32[2,128]{1,0:T(2,128)} %bitcast.29, s32[2,4]{1,0:T(2,128)} %bitcast.30, s32[2,128]{1,0:T(2,128)} %bitcast.31, f32[2,128]{1,0:T(2,128)} %bitcast.32, s32[2,4]{1,0:T(2,128)} %bitcast.33, bf16[128,7168]{1,0:T(8,128)(2,1)} %bitcast.25, ...), custom_call_target="tpu_custom_call" | custom-call | flops 18790481920 | bytes 60000000 | tf_op jit(solution)/shard_map/pallas_call | solution.py:342
  216.9 0.0 copy-start
  217.0 3.0 %copy.15 = bf16[1,128,7168]{2,1,0:T(8,128)(2,1)} copy(bf16[1,128,7168]{2,1,0:T(8,128)(2,1)} %bitcast.22) | data formatting | bytes 3670016
  219.9 0.0 copy-done
  219.9 1.2 copy.16
Async XLA Ops:
  216.9 3.0 %copy-start = (bf16[128,7168]{1,0:T(8,128)(2,1)S(1)}, bf16[128,7168]{1,0:T(8,128)(2,1)}, u32[]{:S(2)}) copy-start(bf16[128,7168]{1,0:T(8,128)(2,1)} %get-tuple-element.5) | copy-start | bytes 5505028

commit v4 on v3

--- a/solution.py
+++ b/solution.py
@@ -12,6 +12,8 @@
 inv_root_tau = 0.3989422804014327
 MESH = pl.DeviceIdType.MESH
 CHUNK = 512
+CUTS = 2
+LAG = 3
 
 
 def gelu_value(h):
@@ -101,21 +103,15 @@
         lax.fori_loop(0, steps, lambda j, _: (body(j), 0)[1], 0)
 
     loop(lambda j: load_rows(0, j).start())
-    load_in.start()
-    loop(lambda j: load_rows(1, j).start())
-    load_out.start()
-    for copy in load_pre:
-        copy.start()
 
     count = metas.shape[2]
     places = lax.broadcasted_iota(jnp.int32, (rows, count), 0).astype(jnp.float32)
-    for m, (ids, gates, words) in enumerate(
-        ((ids_one, gates_one, drop_one), (ids_two, gates_two, drop_two))
-    ):
+
+    def place_rows(m, ids, gates, words):
         seats = routing(ids[...], owners, cap)
-        weights = coefficients(words[...], gates[...])
         mine = [places == seat for seat in seats]
         put[m] = jnp.where(jnp.logical_or(mine[0], mine[1]), 1.0, 0.0).astype(jnp.bfloat16)
+        weights = coefficients(words[...], gates[...])
         for k in range(2):
             metas[0, 4 * m + k : 4 * m + k + 1, :] = seats[k]
         metas[0, 4 * m + 2 : 4 * m + 4, :] = weights
@@ -124,8 +120,8 @@
                 jnp.where(mine[0], weights[0:1], 0.0) + jnp.where(mine[1], weights[1:2], 0.0),
                 axis=1, keepdims=True,
             )
-    zeros[...] = jnp.zeros_like(zeros)
-
+
+    place_rows(0, ids_one, gates_one, drop_one)
     pl.semaphore_wait(barrier, 2 * owners + jnp.where(sends_on, 1, 0))
 
     gots, others = (got_one, got_two), (other_one, other_two)
@@ -194,7 +190,19 @@
             )
         return part.reshape(owners, cap, width).astype(jnp.bfloat16)
 
-    def give_back(m, j):
+    def piece(h):
+        return slice(h * width // CUTS, (h + 1) * width // CUTS)
+
+    def send_back(m, j, s, at):
+        for d in range(owners):
+            to = lax.rem(me + d, owners)
+            pltpu.make_async_remote_copy(
+                gots[m].at[j, 0, to, :, at], backs[m].at[j, me, :, at],
+                c_send.at[m, s], c_recv.at[m, s],
+                device_id=(across, to, core), device_id_type=MESH,
+            ).start()
+
+    def give_back(m, j, cut=False):
         gots[m][j, 1] = project(m, j, 1)
         cross(m, j).start()
         part = project(m, j, 0)
@@ -202,28 +210,32 @@
         gots[m][j, 0] = (
             part.astype(jnp.float32) + others[m][j].astype(jnp.float32)
         ).astype(jnp.bfloat16)
-        for d in range(owners):
-            to = lax.rem(me + d, owners)
-            pltpu.make_async_remote_copy(
-                gots[m].at[j, 0, to], backs[m].at[j, me], c_send.at[m, j], c_recv.at[m, j],
-                device_id=(across, to, core), device_id_type=MESH,
-            ).start()
-
-    def out_local(m, j):
-        return pltpu.make_async_copy(staged.at[m, j], outs[m].at[:, columns(j)], o_send.at[m, j])
-
-    def out_zero(m, j):
-        return pltpu.make_async_copy(zeros, outs[m].at[:, columns(j)], o_recv.at[m, j])
-
-    def out_on(m, j):
+        if cut:
+            for h in range(CUTS):
+                send_back(m, j, j + h, piece(h))
+        else:
+            send_back(m, j, j, slice(None))
+
+    def place(m, j, at):
+        size = len(range(*at.indices(width)))
+        return outs[m].at[:, pl.ds(pl.multiple_of(j * width + (at.start or 0), size), size)]
+
+    def out_local(m, j, s, at):
+        return pltpu.make_async_copy(staged.at[m, j, :, at], place(m, j, at), o_send.at[m, s])
+
+    def out_zero(m, j, s, at):
+        return pltpu.make_async_copy(zeros.at[:, at], place(m, j, at), o_recv.at[m, s])
+
+    def out_on(m, j, s, at):
         return pltpu.make_async_remote_copy(
-            staged.at[m, j], outs[m].at[:, columns(j)], o_send.at[m, j], o_recv.at[m, j],
+            staged.at[m, j, :, at], place(m, j, at), o_send.at[m, s], o_recv.at[m, s],
             device_id=(lax.rem(p + 2, sections), me, core), device_id_type=MESH,
         )
 
-    def collect(m, j):
-        whole(backs[m].at[j], c_recv.at[m, j]).wait()
-        block = flat(backs[m].at[j])
+    def collect(m, j, s=None, at=slice(None)):
+        s = j if s is None else s
+        whole(backs[m].at[j, :, :, at], c_recv.at[m, s]).wait()
+        block = backs[m][j, :, :, at].reshape(rows, -1)
 
         def rows_of(n):
             return jnp.dot(hot[n], block, preferred_element_type=jnp.float32)
@@ -232,25 +244,33 @@
             total = coef[0] * rows_of(0) + coef[1] * rows_of(1)
         else:
             total = rows_of(2)
-        staged[m, j] = total.astype(jnp.bfloat16)
+        staged[m, j, :, at] = total.astype(jnp.bfloat16)
 
         @pl.when(odd == 1)
         def _():
-            out_local(m, j).start()
+            out_local(m, j, s, at).start()
 
         @pl.when(sends_on)
         def _():
-            out_on(m, j).start()
+            out_on(m, j, s, at).start()
 
         @pl.when(p == 0)
         def _():
-            out_zero(m, j).start()
+            out_zero(m, j, s, at).start()
 
     meta_far = pltpu.make_async_remote_copy(
         metas.at[0], metas.at[1], meta_sem.at[0], meta_sem.at[1],
         device_id=(across, me, core), device_id_type=MESH,
     )
-    loop(lambda j: dispatch(0, j))
+    dispatch(0, 0)
+    load_in.start()
+    loop(lambda j: load_rows(1, j).start())
+    load_out.start()
+    for copy in load_pre:
+        copy.start()
+    lax.fori_loop(1, steps, lambda j, _: (dispatch(0, j), 0)[1], 0)
+    place_rows(1, ids_two, gates_two, drop_two)
+    zeros[...] = jnp.zeros_like(zeros)
     meta_far.start()
     acc[...] = jnp.zeros_like(acc)
     load_in.wait()
@@ -289,31 +309,69 @@
         give_back(1, j)
         collect(0, j)
 
-    loop(third)
-    loop(lambda j: collect(1, j))
-
-    def drain(j):
-        for m in range(2):
-            part = gots[m].at[j, 0]
-            whole(part, c_send.at[m, j]).wait()
-
-            @pl.when(odd == 1)
-            def _():
-                out_local(m, j).wait()
-
-            @pl.when(sends_on)
-            def _():
-                out_on(m, j).wait_send()
-
-            @pl.when(gets_on)
-            def _():
-                out_on(m, j).wait_recv()
-
-            @pl.when(p == 0)
-            def _():
-                out_zero(m, j).wait()
-
-    loop(drain)
+    last = steps - 1
+    lax.fori_loop(0, last, lambda j, _: (third(j), 0)[1], 0)
+    give_back(1, last, True)
+    collect(0, last)
+    def drain(m, j, s, at):
+        whole(gots[m].at[j, 0, :, :, at], c_send.at[m, s]).wait()
+
+        @pl.when(odd == 1)
+        def _():
+            out_local(m, j, s, at).wait()
+
+        @pl.when(sends_on)
+        def _():
+            out_on(m, j, s, at).wait_send()
+
+        @pl.when(gets_on)
+        def _():
+            out_on(m, j, s, at).wait_recv()
+
+        @pl.when(p == 0)
+        def _():
+            out_zero(m, j, s, at).wait()
+
+    def fourth(j):
+        collect(1, j)
+        drain(0, j, j, slice(None))
+
+        @pl.when(j >= LAG)
+        def _():
+            drain(1, j - LAG, j - LAG, slice(None))
+
+    lax.fori_loop(0, last, lambda j, _: (fourth(j), 0)[1], 0)
+    drain(0, last, last, slice(None))
+    for h in range(CUTS):
+        collect(1, last, last + h, piece(h))
+    for j in range(last - LAG, last):
+        drain(1, j, j, slice(None))
+    for h in range(CUTS):
+        drain(1, last, last + h, piece(h))
+
+
+def move(one, two, out_one, out_two, held, sem_in, sem_out):
+    part = one.shape[0] // 4
+    pieces = [
+        (n, i, pl.ds(i * part, part), refs)
+        for n, refs in enumerate(((one, out_one), (two, out_two)))
+        for i in range(4)
+    ]
+    loads = [
+        pltpu.make_async_copy(a.at[at], held.at[n, at], sem_in.at[n, i])
+        for n, i, at, (a, _) in pieces
+    ]
+    stores = [
+        pltpu.make_async_copy(held.at[n, at], b.at[at], sem_out.at[n, i])
+        for n, i, at, (_, b) in pieces
+    ]
+    for copy in loads:
+        copy.start()
+    for load, store in zip(loads, stores):
+        load.wait()
+        store.start()
+    for copy in stores:
+        copy.wait()
 
 
 def local(
@@ -369,7 +427,7 @@
             dma((4,)),
             dma((2,)),
         ]
-        + [dma((2, steps))] * 11,
+        + [dma((2, steps + CUTS))] * 11,
         compiler_params=pltpu.CompilerParams(
             collective_id=0, has_side_effects=True, vmem_limit_bytes=62 << 20
         ),
@@ -389,6 +447,13 @@
         w_in[0, 0],
         w_out[0, 0],
     )
+    result = pl.pallas_call(
+        move,
+        out_shape=(jax.ShapeDtypeStruct((count, model), b16),) * 2,
+        in_specs=[hbm] * 2,
+        out_specs=(hbm,) * 2,
+        scratch_shapes=[pltpu.VMEM((2, count, model), b16), dma((2, 4)), dma((2, 4))],
+    )(*result)
     return (result[0][None], result[1][None])
 
 

time: 221 us -> 220 us (level)
  local copies, waits for them, and re-layouts: 4.21 us -> 0 us
  Pallas kernels: 216 us -> 219 us
    unnamed x4 -> x0, local copies, waits for them, and re-layouts: 4.21 us -> none
    pallas_call x0 -> x1, Pallas kernels: none -> 3.06 us  [local(): pl.pallas_call(move, out_shape=(jax.ShapeDtypeStruct((count, model), b16)...]
where the time goes in v4:
time: 220 us
  Pallas kernels  219 us (100%)
    pallas_call x1, Pallas kernels, local(): pl.pallas_call(functools.partial(relay, (owners, cap, steps, width, secti...  216 us

profile of v4, /device:TPU:24, one launch (start us, length us, event | category | flops | bytes accessed | tf_op | source)
XLA Modules:
  0.0 219.9 jit_solution(11501916733720370468)
XLA Ops:
  0.6 216.2 %shard_map.122 = (bf16[128,7168]{1,0:T(8,128)(2,1)}, bf16[128,7168]{1,0:T(8,128)(2,1)}) custom-call(s32[2,128]{1,0:T(2,128)} %bitcast.28, f32[2,128]{1,0:T(2,128)} %bitcast.29, s32[2,4]{1,0:T(2,128)} %bitcast.30, s32[2,128]{1,0:T(2,128)} %bitcast.31, f32[2,128]{1,0:T(2,128)} %bitcast.32, s32[2,4]{1,0:T(2,128)} %bitcast.33, bf16[128,7168]{1,0:T(8,128)(2,1)} %bitcast.23, ...), custom_call_target="tpu_custom_call" | custom-call | flops 18790481920 | bytes 60000000 | tf_op jit(solution)/shard_map/pallas_call | solution.py:400
  216.9 3.1 %shard_map.123 = (bf16[128,7168]{1,0:T(8,128)(2,1)}, bf16[128,7168]{1,0:T(8,128)(2,1)}) custom-call(bf16[128,7168]{1,0:T(8,128)(2,1)} %get-tuple-element.6.one, bf16[128,7168]{1,0:T(8,128)(2,1)} %get-tuple-element.7.two), custom_call_target="tpu_custom_call" | custom-call | tf_op jit(solution)/shard_map/pallas_call | solution.py:450

commit v5 on v4

--- a/solution.py
+++ b/solution.py
@@ -14,6 +14,7 @@
 CHUNK = 512
 CUTS = 2
 LAG = 3
+DIRECT = 1
 
 
 def gelu_value(h):
@@ -67,6 +68,8 @@
     p, me, core = lax.axis_index("pipe"), lax.axis_index("expert"), lax.axis_index("dp")
     odd = lax.rem(p, 2)
     across = p + 1 - 2 * odd
+    onward = lax.rem(p + 1, sections)
+    has_next, has_prior = p + 1 < sections, p >= 1
     sends_on = jnp.logical_and(odd == 0, p + 2 < sections)
     gets_on = jnp.logical_and(odd == 0, p >= 2)
 
@@ -84,6 +87,10 @@
     @pl.when(gets_on)
     def _():
         pl.semaphore_signal(barrier, device_id=(p - 2, me, core), device_id_type=MESH)
+        for d in range(owners):
+            pl.semaphore_signal(
+                barrier, device_id=(p - 1, lax.rem(me + d, owners), core), device_id_type=MESH
+            )
 
     load_in = pltpu.make_async_copy(w_in, wi, load_sem.at[0])
     load_out = pltpu.make_async_copy(w_out, wo, load_sem.at[1])
@@ -122,7 +129,12 @@
             )
 
     place_rows(0, ids_one, gates_one, drop_one)
-    pl.semaphore_wait(barrier, 2 * owners + jnp.where(sends_on, 1, 0))
+    pl.semaphore_wait(
+        barrier,
+        2 * owners
+        + jnp.where(sends_on, 1, 0)
+        + jnp.where(jnp.logical_and(odd == 1, has_next), owners, 0),
+    )
 
     gots, others = (got_one, got_two), (other_one, other_two)
     backs, outs = (back_one, back_two), (out_one, out_two)
@@ -193,13 +205,13 @@
     def piece(h):
         return slice(h * width // CUTS, (h + 1) * width // CUTS)
 
-    def send_back(m, j, s, at):
+    def send_back(m, j, s, at, section=None):
         for d in range(owners):
             to = lax.rem(me + d, owners)
             pltpu.make_async_remote_copy(
                 gots[m].at[j, 0, to, :, at], backs[m].at[j, me, :, at],
                 c_send.at[m, s], c_recv.at[m, s],
-                device_id=(across, to, core), device_id_type=MESH,
+                device_id=(across if section is None else section, to, core), device_id_type=MESH,
             ).start()
 
     def give_back(m, j, cut=False):
@@ -212,7 +224,13 @@
         ).astype(jnp.bfloat16)
         if cut:
             for h in range(CUTS):
-                send_back(m, j, j + h, piece(h))
+                if h < DIRECT:
+                    send_back(m, j, j + h, piece(h))
+                else:
+
+                    @pl.when(has_next)
+                    def _():
+                        send_back(m, j, j + h, piece(h), onward)
         else:
             send_back(m, j, j, slice(None))
 
@@ -231,6 +249,32 @@
             staged.at[m, j, :, at], place(m, j, at), o_send.at[m, s], o_recv.at[m, s],
             device_id=(lax.rem(p + 2, sections), me, core), device_id_type=MESH,
         )
+
+    def collect_direct(m, j, s, at):
+        @pl.when(has_prior)
+        def _():
+            whole(backs[m].at[j, :, :, at], c_recv.at[m, s]).wait()
+            block = backs[m][j, :, :, at].reshape(rows, -1)
+            total = jnp.dot(hot[3], block, preferred_element_type=jnp.float32)
+            staged[m, j, :, at] = total.astype(jnp.bfloat16)
+            out_local(m, j, s, at).start()
+
+        @pl.when(p == 0)
+        def _():
+            out_zero(m, j, s, at).start()
+
+    def drain_direct(m, j, s, at):
+        @pl.when(has_next)
+        def _():
+            whole(gots[m].at[j, 0, :, :, at], c_send.at[m, s]).wait()
+
+        @pl.when(has_prior)
+        def _():
+            out_local(m, j, s, at).wait()
+
+        @pl.when(p == 0)
+        def _():
+            out_zero(m, j, s, at).wait()
 
     def collect(m, j, s=None, at=slice(None)):
         s = j if s is None else s
@@ -272,6 +316,15 @@
     place_rows(1, ids_two, gates_two, drop_two)
     zeros[...] = jnp.zeros_like(zeros)
     meta_far.start()
+    meta_on = pltpu.make_async_remote_copy(
+        metas.at[0], metas.at[2], meta_sem.at[2], meta_sem.at[3],
+        device_id=(onward, me, core), device_id_type=MESH,
+    )
+
+    @pl.when(has_next)
+    def _():
+        meta_on.start()
+
     acc[...] = jnp.zeros_like(acc)
     load_in.wait()
 
@@ -297,13 +350,25 @@
     meta_far.wait()
     seat_at = lax.broadcasted_iota(jnp.int32, (count, rows), 1).astype(jnp.float32)
 
-    def theirs(n):
-        return seat_at == upright(metas[1, n : n + 1, :])
+    def theirs(n, slot=1):
+        return seat_at == upright(metas[slot, n : n + 1, :])
 
     for k in range(2):
         hot[k] = jnp.where(theirs(k), 1.0, 0.0).astype(jnp.bfloat16)
         coef[k] = upright(metas[1, 2 + k : 3 + k, :])
     hot[2] = jnp.where(jnp.logical_or(theirs(4), theirs(5)), 1.0, 0.0).astype(jnp.bfloat16)
+
+    @pl.when(has_next)
+    def _():
+        meta_on.wait_send()
+
+    @pl.when(has_prior)
+    def _():
+        meta_on.wait_recv()
+        hot[3] = jnp.where(
+            jnp.logical_or(theirs(4, 2), theirs(5, 2)), 1.0, 0.0
+        ).astype(jnp.bfloat16)
+
 
     def third(j):
         give_back(1, j)
@@ -343,11 +408,11 @@
     lax.fori_loop(0, last, lambda j, _: (fourth(j), 0)[1], 0)
     drain(0, last, last, slice(None))
     for h in range(CUTS):
-        collect(1, last, last + h, piece(h))
+        (collect if h < DIRECT else collect_direct)(1, last, last + h, piece(h))
     for j in range(last - LAG, last):
         drain(1, j, j, slice(None))
     for h in range(CUTS):
-        drain(1, last, last + h, piece(h))
+        (drain if h < DIRECT else drain_direct)(1, last, last + h, piece(h))
 
 
 def move(one, two, out_one, out_two, held, sem_in, sem_out):
@@ -417,15 +482,15 @@
             pltpu.VMEM((2, 2, rows, half), f32),
             pltpu.VMEM((2, 2, rows, half), b16),
             pltpu.VMEM((2, owners, cap, half), b16),
-            pltpu.VMEM((2, 8, count), f32),
+            pltpu.VMEM((3, 8, count), f32),
             pltpu.VMEM((count, width), b16),
             pltpu.VMEM((2, steps, count, width), b16),
             pltpu.VMEM((2, rows, count), b16),
             pltpu.VMEM((rows, 1), f32),
-            pltpu.VMEM((3, count, rows), b16),
+            pltpu.VMEM((4, count, rows), b16),
             pltpu.VMEM((2, count, 1), f32),
             dma((4,)),
-            dma((2,)),
+            dma((4,)),
         ]
         + [dma((2, steps + CUTS))] * 11,
         compiler_params=pltpu.CompilerParams(

time: 220 us -> 219 us (level)
  no operation moved by 1% of the time
where the time goes in v5:
time: 219 us
  Pallas kernels  218 us (100%)
    pallas_call x1, Pallas kernels, local(): pl.pallas_call(functools.partial(relay, (owners, cap, steps, width, secti...  215 us

profile of v5, /device:TPU:24, one launch (start us, length us, event | category | flops | bytes accessed | tf_op | source)
XLA Modules:
  0.0 218.9 jit_solution(3118714101703227111)
XLA Ops:
  0.6 215.2 %shard_map.122 = (bf16[128,7168]{1,0:T(8,128)(2,1)}, bf16[128,7168]{1,0:T(8,128)(2,1)}) custom-call(s32[2,128]{1,0:T(2,128)} %bitcast.28, f32[2,128]{1,0:T(2,128)} %bitcast.29, s32[2,4]{1,0:T(2,128)} %bitcast.30, s32[2,128]{1,0:T(2,128)} %bitcast.31, f32[2,128]{1,0:T(2,128)} %bitcast.32, s32[2,4]{1,0:T(2,128)} %bitcast.33, bf16[128,7168]{1,0:T(8,128)(2,1)} %bitcast.23, ...), custom_call_target="tpu_custom_call" | custom-call | flops 18790481920 | bytes 60000000 | tf_op jit(solution)/shard_map/pallas_call | solution.py:465
  215.8 3.1 %shard_map.123 = (bf16[128,7168]{1,0:T(8,128)(2,1)}, bf16[128,7168]{1,0:T(8,128)(2,1)}) custom-call(bf16[128,7168]{1,0:T(8,128)(2,1)} %get-tuple-element.6.one, bf16[128,7168]{1,0:T(8,128)(2,1)} %get-tuple-element.7.two), custom_call_target="tpu_custom_call" | custom-call | tf_op jit(solution)/shard_map/pallas_call | solution.py:515
